TPU v7x, 32 devices: a whole 2x2x4 slice. The times are simulated.
32 devices in a mesh: dp: 8 (over z, y), ctx: 2 (over x), tp: 2 (over core).
Axes of the slice: x: 2, y: 2, z: 4, core: 2. Of those that a mesh axis runs over, the one named last changes fastest.
Arguments:
- hidden_in: bfloat16 [8192, 1024], P(('dp', 'ctx')), may hold values from -6 to 6
- encoder_states: bfloat16 [4096, 1024], P(('dp', 'ctx')), may hold values from -6 to 6
- out_grad: bfloat16 [8192, 1024], P(('dp', 'ctx')), may hold values from -6 to 6
- target_ids: int32 [8, 1024], P('dp'), may hold values from 0 to 3, never falling along the last dimension, each value on 1 to 800 neighbouring positions
- source_ids: int32 [8, 512], P('dp'), may hold values from 0 to 3, never falling along the last dimension, each value on 1 to 400 neighbouring positions
- self_in: bfloat16 [3, 1024, 1024], P(None, 'dp', 'tp'), may hold values from -0.1875 to 0.1875
- self_out: bfloat16 [1024, 1024], P('tp', 'dp'), may hold values from -1.5 to 1.5
- cross_in: bfloat16 [3, 1024, 1024], P(None, 'dp', 'tp'), may hold values from -0.1875 to 0.1875
- cross_out: bfloat16 [1024, 1024], P('tp', 'dp'), may hold values from -1.5 to 1.5
- ffn_in: bfloat16 [1024, 8192], P('dp', 'tp'), may hold values from -0.1875 to 0.1875
- ffn_out: bfloat16 [8192, 1024], P('tp', 'dp'), may hold values from -0.0625 to 0.0625
- norm_gain: bfloat16 [3, 1024], P(None, 'dp'), may hold values from 0.25 to 1.75
- norm_bias: bfloat16 [3, 1024], P(None, 'dp'), may hold values from -3 to 3
Outputs:
- out_hidden: bfloat16 [8192, 1024], P(('dp', 'ctx'))
- grad_hidden: float32 [8192, 1024], P(('dp', 'ctx'))
- grad_encoder: float32 [4096, 1024], P(('dp', 'ctx'))
- grad_self_in: float32 [3, 1024, 1024], P(None, 'dp', 'tp')
- grad_self_out: float32 [1024, 1024], P('tp', 'dp')
- grad_cross_in: float32 [3, 1024, 1024], P(None, 'dp', 'tp')
- grad_cross_out: float32 [1024, 1024], P('tp', 'dp')
- grad_ffn_in: float32 [1024, 8192], P('dp', 'tp')
- grad_ffn_out: float32 [8192, 1024], P('tp', 'dp')
- grad_norm_gain: float32 [3, 1024], P(None, 'dp')
- grad_norm_bias: float32 [3, 1024], P(None, 'dp')
Inputs may be any that keep to these rules, and one draw needn't show every extreme that they name: `target_ids`: along each sequence the ids never fall; each of the 4 documents holds 1 to 800 decoder positions, and one holds exactly 800. `source_ids`: along each sequence the ids never fall; each of the 4 documents holds 1 to 400 encoder positions, and one holds exactly 400.
All inputs are finite; a program needn't handle non-finite values.
Results may differ from a plain program's by a relative error of at most 0.018.
Values may be sent and summed in bfloat16 or wider, within the bound.
No kernel may reach another device: no remote copies, remote signals or barrier semaphores. Data moves between devices by JAX's collectives and lax.ppermute only.
A program may use at most 256 MiB of HBM per device.

v0:
```python
import jax
import jax.numpy as jnp
from jax import lax
from jax.sharding import PartitionSpec as P

HEAD_DIM = 64


epsilon = 1e-05
masked_score = -1000000000.0


def product(left, right):
    return jnp.dot(left, right, preferred_element_type=jnp.float32)


def left_product(left, right):
    return lax.dot_general(
        left, right, (((0,), (0,)), ((), ())), preferred_element_type=jnp.float32
    )


def right_product(left, right):
    return lax.dot_general(
        left, right, (((1,), (1,)), ((), ())), preferred_element_type=jnp.float32
    )


def gelu_tanh(values):
    return jax.nn.gelu(values, approximate=True)


def norm_forward(values, gain, shift):
    centre = jnp.mean(values, axis=-1, keepdims=True)
    centred = values - centre
    factor = lax.rsqrt(jnp.mean(centred * centred, axis=-1, keepdims=True) + epsilon)
    normal = centred * factor
    return (normal * gain + shift, normal, factor)


def norm_backward(grad_norm, normal, factor, gain):
    scaled = grad_norm * gain
    inner = (
        scaled
        - jnp.mean(scaled, axis=-1, keepdims=True)
        - normal * jnp.mean(scaled * normal, axis=-1, keepdims=True)
    )
    return (factor * inner, jnp.sum(grad_norm * normal, axis=0), jnp.sum(grad_norm, axis=0))


def split_heads(values):
    return values.reshape(values.shape[0], values.shape[1] // HEAD_DIM, HEAD_DIM)


def masked_scores(queries, key_rows, allowed):
    scores = jnp.einsum(
        "qhd,khd->hqk",
        split_heads(queries),
        split_heads(key_rows),
        preferred_element_type=jnp.float32,
    )
    return jnp.where(allowed[None], scores * HEAD_DIM ** (-0.5), masked_score)


def attend_forward(queries, key_rows, value_rows, allowed):
    scores = masked_scores(queries, key_rows, allowed)
    peak = jnp.max(scores, axis=-1, keepdims=True)
    expo = jnp.exp(scores - peak)
    total = jnp.sum(expo, axis=-1, keepdims=True)
    probs = (expo / total).astype(jnp.bfloat16)
    mixed = jnp.einsum(
        "hqk,khd->qhd", probs, split_heads(value_rows), preferred_element_type=jnp.float32
    )
    return (
        mixed.reshape(queries.shape[0], queries.shape[1]).astype(jnp.bfloat16),
        peak + jnp.log(total),
    )


def attend_backward(grad_mixed, queries, key_rows, value_rows, allowed, log_total):
    scores = masked_scores(queries, key_rows, allowed)
    probs = jnp.exp(scores - log_total)
    grad_heads = split_heads(grad_mixed)
    grad_values = jnp.einsum(
        "hqk,qhd->khd", probs.astype(jnp.bfloat16), grad_heads, preferred_element_type=jnp.float32
    )
    grad_probs = jnp.einsum(
        "qhd,khd->hqk", grad_heads, split_heads(value_rows), preferred_element_type=jnp.float32
    )
    grad_scores = probs * (grad_probs - jnp.sum(probs * grad_probs, axis=-1, keepdims=True))
    grad_scores = grad_scores.astype(jnp.bfloat16)
    grad_queries = jnp.einsum(
        "hqk,khd->qhd", grad_scores, split_heads(key_rows), preferred_element_type=jnp.float32
    ) * HEAD_DIM ** (-0.5)
    grad_keys = jnp.einsum(
        "hqk,qhd->khd", grad_scores, split_heads(queries), preferred_element_type=jnp.float32
    ) * HEAD_DIM ** (-0.5)
    return (
        grad_queries.reshape(queries.shape),
        grad_keys.reshape(key_rows.shape),
        grad_values.reshape(value_rows.shape),
    )


def branch_sum(partial_rows):
    return lax.psum(partial_rows, "tp")


def input_sum(partials):
    return lax.psum(partials, "tp")


def per_device(
    hidden_in,
    encoder_states,
    out_grad,
    target_ids,
    source_ids,
    self_in,
    self_out,
    cross_in,
    cross_out,
    ffn_in,
    ffn_out,
    norm_gain,
    norm_bias,
):
    local_rows = hidden_in.shape[0]
    first_row = lax.axis_index("ctx") * local_rows
    target_row = target_ids[0]
    source_row = source_ids[0]
    query_ids = lax.dynamic_slice_in_dim(target_row, first_row, local_rows)
    query_place = first_row + jnp.arange(local_rows, dtype=jnp.int32)
    key_place = jnp.arange(target_row.shape[0], dtype=jnp.int32)
    self_allowed = (query_ids[:, None] == target_row[None, :]) & (
        key_place[None, :] <= query_place[:, None]
    )
    cross_allowed = query_ids[:, None] == source_row[None, :]
    fetched = (
        lax.all_gather(self_in, "dp", axis=1, tiled=True),
        lax.all_gather(self_out, "dp", axis=1, tiled=True),
        lax.all_gather(cross_in, "dp", axis=1, tiled=True),
        lax.all_gather(cross_out, "dp", axis=1, tiled=True),
        lax.all_gather(ffn_in, "dp", axis=0, tiled=True),
        lax.all_gather(ffn_out, "dp", axis=1, tiled=True),
        lax.all_gather(norm_gain, "dp", axis=1, tiled=True),
        lax.all_gather(norm_bias, "dp", axis=1, tiled=True),
    )
    self_w, self_o, cross_w, cross_o, up_w, down_w, gains, biases = fetched
    gains = gains.astype(jnp.float32)
    biases = biases.astype(jnp.float32)
    start_rows = hidden_in.astype(jnp.float32)
    normed, normal_one, factor_one = norm_forward(start_rows, gains[0], biases[0])
    input_one = normed.astype(jnp.bfloat16)
    queries = product(input_one, self_w[0]).astype(jnp.bfloat16)
    key_self = product(input_one, self_w[1]).astype(jnp.bfloat16)
    value_self = product(input_one, self_w[2]).astype(jnp.bfloat16)
    key_cross = product(encoder_states, cross_w[1]).astype(jnp.bfloat16)
    value_cross = product(encoder_states, cross_w[2]).astype(jnp.bfloat16)
    key_self, value_self, key_cross, value_cross = (
        lax.all_gather(key_self, "ctx", axis=0, tiled=True),
        lax.all_gather(value_self, "ctx", axis=0, tiled=True),
        lax.all_gather(key_cross, "ctx", axis=0, tiled=True),
        lax.all_gather(value_cross, "ctx", axis=0, tiled=True),
    )
    mixed_one, total_one = attend_forward(queries, key_self, value_self, self_allowed)
    first_rows = start_rows + branch_sum(product(mixed_one, self_o))
    normed, normal_two, factor_two = norm_forward(first_rows, gains[1], biases[1])
    input_two = normed.astype(jnp.bfloat16)
    cross_queries = product(input_two, cross_w[0]).astype(jnp.bfloat16)
    mixed_two, total_two = attend_forward(cross_queries, key_cross, value_cross, cross_allowed)
    second_rows = first_rows + branch_sum(product(mixed_two, cross_o))
    normed, normal_three, factor_three = norm_forward(second_rows, gains[2], biases[2])
    input_three = normed.astype(jnp.bfloat16)
    activated, gelu_pull = jax.vjp(gelu_tanh, product(input_three, up_w))
    activated = activated.astype(jnp.bfloat16)
    result = (second_rows + branch_sum(product(activated, down_w))).astype(jnp.bfloat16)
    grad_rows = out_grad.astype(jnp.float32)
    grad_down = left_product(activated, out_grad)
    grad_up = gelu_pull(right_product(out_grad, down_w))[0].astype(jnp.bfloat16)
    grad_ffn = left_product(input_three, grad_up)
    grad_norm = input_sum((right_product(grad_up, up_w),))[0]
    grad_back, gain_three, bias_three = norm_backward(
        grad_norm, normal_three, factor_three, gains[2]
    )
    grad_second = grad_rows + grad_back
    grad_branch = grad_second.astype(jnp.bfloat16)
    grad_cross_o = left_product(mixed_two, grad_branch)
    grad_mixed = right_product(grad_branch, cross_o).astype(jnp.bfloat16)
    grad_cq, grad_ck, grad_cv = attend_backward(
        grad_mixed, cross_queries, key_cross, value_cross, cross_allowed, total_two
    )
    grad_cq = grad_cq.astype(jnp.bfloat16)
    grad_cross_q = left_product(input_two, grad_cq)
    grad_norm = input_sum((right_product(grad_cq, cross_w[0]),))[0]
    grad_back, gain_two, bias_two = norm_backward(grad_norm, normal_two, factor_two, gains[1])
    grad_first = grad_second + grad_back
    grad_branch = grad_first.astype(jnp.bfloat16)
    grad_self_o = left_product(mixed_one, grad_branch)
    grad_mixed = right_product(grad_branch, self_o).astype(jnp.bfloat16)
    grad_sq, grad_sk, grad_sv = attend_backward(
        grad_mixed, queries, key_self, value_self, self_allowed, total_one
    )
    grad_sq = grad_sq.astype(jnp.bfloat16)
    grad_sk, grad_sv, grad_ck, grad_cv = (
        lax.psum_scatter(
            grad_sk.astype(jnp.bfloat16), "ctx", scatter_dimension=0, tiled=True
        ).astype(jnp.float32),
        lax.psum_scatter(
            grad_sv.astype(jnp.bfloat16), "ctx", scatter_dimension=0, tiled=True
        ).astype(jnp.float32),
        lax.psum_scatter(
            grad_ck.astype(jnp.bfloat16), "ctx", scatter_dimension=0, tiled=True
        ).astype(jnp.float32),
        lax.psum_scatter(
            grad_cv.astype(jnp.bfloat16), "ctx", scatter_dimension=0, tiled=True
        ).astype(jnp.float32),
    )
    grad_sk = grad_sk.astype(jnp.bfloat16)
    grad_sv = grad_sv.astype(jnp.bfloat16)
    grad_ck = grad_ck.astype(jnp.bfloat16)
    grad_cv = grad_cv.astype(jnp.bfloat16)
    grad_self_in = jnp.stack(
        [
            left_product(input_one, grad_sq),
            left_product(input_one, grad_sk),
            left_product(input_one, grad_sv),
        ]
    )
    grad_cross_in = jnp.stack(
        [grad_cross_q, left_product(encoder_states, grad_ck), left_product(encoder_states, grad_cv)]
    )
    self_part = (
        right_product(grad_sq, self_w[0])
        + right_product(grad_sk, self_w[1])
        + right_product(grad_sv, self_w[2])
    )
    source_part = right_product(grad_ck, cross_w[1]) + right_product(grad_cv, cross_w[2])
    grad_norm, grad_source = input_sum((self_part, source_part))
    grad_back, gain_one, bias_one = norm_backward(grad_norm, normal_one, factor_one, gains[0])
    grad_input = grad_first + grad_back
    grad_gains = jnp.stack([gain_one, gain_two, gain_three])
    grad_biases = jnp.stack([bias_one, bias_two, bias_three])
    shards = (
        lax.psum_scatter(grad_self_in, "dp", scatter_dimension=1, tiled=True),
        lax.psum_scatter(grad_self_o, "dp", scatter_dimension=1, tiled=True),
        lax.psum_scatter(grad_cross_in, "dp", scatter_dimension=1, tiled=True),
        lax.psum_scatter(grad_cross_o, "dp", scatter_dimension=1, tiled=True),
        lax.psum_scatter(grad_ffn, "dp", scatter_dimension=0, tiled=True),
        lax.psum_scatter(grad_down, "dp", scatter_dimension=1, tiled=True),
        lax.psum_scatter(grad_gains, "dp", scatter_dimension=1, tiled=True),
        lax.psum_scatter(grad_biases, "dp", scatter_dimension=1, tiled=True),
    )
    shards = (
        lax.psum(shards[0].astype(jnp.bfloat16), "ctx").astype(jnp.float32),
        lax.psum(shards[1].astype(jnp.bfloat16), "ctx").astype(jnp.float32),
        lax.psum(shards[2].astype(jnp.bfloat16), "ctx").astype(jnp.float32),
        lax.psum(shards[3].astype(jnp.bfloat16), "ctx").astype(jnp.float32),
        lax.psum(shards[4].astype(jnp.bfloat16), "ctx").astype(jnp.float32),
        lax.psum(shards[5].astype(jnp.bfloat16), "ctx").astype(jnp.float32),
        lax.psum(shards[6].astype(jnp.bfloat16), "ctx").astype(jnp.float32),
        lax.psum(shards[7].astype(jnp.bfloat16), "ctx").astype(jnp.float32),
    )
    return (
        result,
        grad_input,
        grad_source,
        shards[0],
        shards[1],
        shards[2],
        shards[3],
        shards[4],
        shards[5],
        shards[6],
        shards[7],
    )


def solution(mesh):
    return jax.shard_map(
        per_device,
        mesh=mesh,
        in_specs=(
            P(("dp", "ctx"), None),
            P(("dp", "ctx"), None),
            P(("dp", "ctx"), None),
            P("dp", None),
            P("dp", None),
            P(None, "dp", "tp"),
            P("tp", "dp"),
            P(None, "dp", "tp"),
            P("tp", "dp"),
            P("dp", "tp"),
            P("tp", "dp"),
            P(None, "dp"),
            P(None, "dp"),
        ),
        out_specs=(
            P(("dp", "ctx"), None),
            P(("dp", "ctx"), None),
            P(("dp", "ctx"), None),
            P(None, "dp", "tp"),
            P("tp", "dp"),
            P(None, "dp", "tp"),
            P("tp", "dp"),
            P("dp", "tp"),
            P("tp", "dp"),
            P(None, "dp"),
            P(None, "dp"),
        ),
        check_vma=False,
    )
```

profile of v0, /device:TPU:0, one launch (start us, length us, event | category | flops | bytes accessed | tf_op | source)
XLA Modules:
  0.0 1967.2 jit_solution(8780536123767302130)
XLA Ops:
  8.0 22.6 %all_gather.36 = bf16[3,1024]{1,0:T(4,128)(2,1)S(1)} all-gather(bf16[3,128]{1,0:T(4,128)(2,1)} %param.24), channel_id=1, replica_groups=mesh['dp'=8,'ctx'=2,'tp'=2] {'dp'}, dimensions={1}, use_global_device_ids=true | all-gather | bytes 6912 | tf_op jit(solution)/shard_map/all_gather | solution.py:146
  30.6 16.8 all_gather.37
  49.3 24.2 %all-gather.9.cloned.1.call-done = bf16[3,1024,512]{2,1,0:T(8,128)(2,1)} async-done(((bf16[3,128,512]{2,1,0:T(8,128)(2,1)}), bf16[3,1024,512]{2,1,0:T(8,128)(2,1)}) %all-gather.9.cloned.1.call-update) | async-done | bytes 3145744 | tf_op jit(solution)/shard_map/all_gather | solution.py:140
  73.5 2.8 convolution_convert_fusion.3
  76.4 2.8 convolution_convert_fusion.5
  84.1 12.3 all-gather.13.cloned.1.call-done
  97.9 22.0 %all-gather.11.cloned.1.call-done = bf16[1024,512]{1,0:T(8,128)(2,1)} async-done(((bf16[512,512]{1,0:T(8,128)(2,1)}), bf16[1024,512]{1,0:T(8,128)(2,1)}) %all-gather.11.cloned.1.call-update) | async-done | bytes 1048592 | tf_op jit(solution)/shard_map/all_gather | solution.py:162
  121.4 4.6 fusion.69
  126.0 3.5 fusion
  132.2 3.8 fusion.44
  136.0 25.4 %all-gather.15.cloned.1.call-done = bf16[512,1024]{1,0:T(8,128)(2,1)} async-done(((bf16[512,128]{1,0:T(8,128)(2,1)}), bf16[512,1024]{1,0:T(8,128)(2,1)}) %all-gather.15.cloned.1.call-update) | async-done | bytes 1048592 | tf_op jit(solution)/shard_map/all_gather | solution.py:141
  161.3 3.3 fusion.71
  166.4 56.4 %all-gather.17.cloned.1.call-done = bf16[3,1024,512]{2,1,0:T(8,128)(2,1)} async-done(((bf16[3,128,512]{2,1,0:T(8,128)(2,1)}), bf16[3,1024,512]{2,1,0:T(8,128)(2,1)}) %all-gather.17.cloned.1.call-update) | async-done | bytes 3145744 | tf_op jit(solution)/shard_map/all_gather | solution.py:142
  224.5 7.9 all_gather.44
  234.5 7.2 all_gather.43
  242.7 2.7 all-reduce.10.cloned.1.call-done
  256.8 31.7 %all-gather.19.cloned.1.call-done = bf16[512,1024]{1,0:T(8,128)(2,1)} async-done(((bf16[512,128]{1,0:T(8,128)(2,1)}), bf16[512,1024]{1,0:T(8,128)(2,1)}) %all-gather.19.cloned.1.call-update) | async-done | bytes 1048592 | tf_op jit(solution)/shard_map/all_gather | solution.py:143
  288.5 3.3 fusion.72
  293.2 18.9 all-reduce.12.cloned.1.call-done
  315.6 125.0 %all-gather.23.cloned.1.call-done = bf16[4096,1024]{1,0:T(8,128)(2,1)} async-done(((bf16[4096,128]{1,0:T(8,128)(2,1)}), bf16[4096,1024]{1,0:T(8,128)(2,1)}) %all-gather.23.cloned.1.call-update) | async-done | bytes 8388624 | tf_op jit(solution)/shard_map/all_gather | solution.py:145
  440.7 11.5 fusion.73
  452.2 113.6 %all-gather.21.cloned.1.call-done = bf16[1024,4096]{1,0:T(8,128)(2,1)} async-done(((bf16[128,4096]{1,0:T(8,128)(2,1)}), bf16[1024,4096]{1,0:T(8,128)(2,1)}) %all-gather.21.cloned.1.call-update) | async-done | bytes 8388624 | tf_op jit(solution)/shard_map/all_gather | solution.py:144
  565.8 18.5 fusion.8
  586.3 5.9 fusion.74
  592.3 19.5 all-reduce.14.cloned.1.call-done
  611.7 3.8 multiply_reduce_fusion.2
  615.6 3.4 multiply_add_fusion.1
  628.7 3.3 fusion.47
  632.1 4.5 fusion.43
  636.7 6.3 fusion.39
  643.1 11.5 all-reduce.16.cloned.1.call-done
  654.6 3.2 multiply_reduce_fusion.3
  661.5 15.0 multiply_reduce_fusion
  678.6 7.9 multiply_convert_fusion
  686.5 3.1 multiply_convert_fusion.3
  690.2 8.6 fusion.34
  698.8 12.2 fusion.58
  711.1 2.8 fusion.48
  713.8 3.2 convolution_add_fusion
  717.0 6.0 fusion.37
  723.9 3.4 fusion.45
  727.2 3.5 fusion.46
  730.7 4.8 reduce-scatter.19.cloned.1.call-done
  735.5 4.8 add_add_fusion
  741.3 3.6 fusion.52
  746.0 4.0 fusion.49
  753.6 3.3 pad_maximum_fusion.1
  761.4 3.6 pad_maximum_fusion
  766.2 15.9 fusion.57
  783.9 10.6 fusion.55
  794.7 2.9 fusion.31
  799.8 44.1 %reduce-scatter.31.cloned.1.call-done = f32[512,128]{1,0:T(8,128)} async-done(((f32[512,1024]{1,0:T(8,128)}), f32[512,128]{1,0:T(8,128)}) %reduce-scatter.31.cloned.1.call-update) | async-done | bytes 262160 | tf_op jit(solution)/shard_map/reduce_scatter | solution.py:248
  845.6 70.1 %reduce-scatter.27.cloned.1.call-done = f32[512,128]{1,0:T(8,128)} async-done(((f32[512,1024]{1,0:T(8,128)}), f32[512,128]{1,0:T(8,128)}) %reduce-scatter.27.cloned.1.call-update) | async-done | bytes 262160 | tf_op jit(solution)/shard_map/reduce_scatter | solution.py:246
  917.3 119.7 %reduce-scatter.29.cloned.1.call-done = f32[3,128,512]{2,1,0:T(8,128)} async-done(((f32[3,1024,512]{2,1,0:T(8,128)}), f32[3,128,512]{2,1,0:T(8,128)}) %reduce-scatter.29.cloned.1.call-update) | async-done | bytes 786448 | tf_op jit(solution)/shard_map/reduce_scatter | solution.py:247
  1039.0 119.6 %reduce-scatter.25.cloned.1.call-done = f32[3,128,512]{2,1,0:T(8,128)} async-done(((f32[3,1024,512]{2,1,0:T(8,128)}), f32[3,128,512]{2,1,0:T(8,128)}) %reduce-scatter.25.cloned.1.call-update) | async-done | bytes 786448 | tf_op jit(solution)/shard_map/reduce_scatter | solution.py:245
  1160.5 284.2 %reduce-scatter.35.cloned.1.call-done = f32[4096,128]{1,0:T(8,128)} async-done(((f32[4096,1024]{1,0:T(8,128)}), f32[4096,128]{1,0:T(8,128)}) %reduce-scatter.35.cloned.1.call-update) | async-done | bytes 2097168 | tf_op jit(solution)/shard_map/reduce_scatter | solution.py:250
  1444.8 2.7 convert_element_type.270
  1447.4 282.9 %reduce-scatter.33.cloned.1.call-done = f32[128,4096]{1,0:T(8,128)} async-done(((f32[1024,4096]{1,0:T(8,128)}), f32[128,4096]{1,0:T(8,128)}) %reduce-scatter.33.cloned.1.call-update) | async-done | bytes 2097168 | tf_op jit(solution)/shard_map/reduce_scatter | solution.py:249
  1730.4 2.7 convert_element_type.268
  1733.1 3.0 add_convert_fusion
  1738.6 56.9 %reduce-scatter.39.cloned.1.call-done = f32[128,3]{1,0:T(8,128)} async-done(((f32[1024,3]{1,0:T(8,128)}), f32[128,3]{1,0:T(8,128)}) %reduce-scatter.39.cloned.1.call-update) | async-done | bytes 1552
  1796.4 63.9 %reduce-scatter.37.cloned.1.call-done = f32[128,3]{1,0:T(8,128)} async-done(((f32[1024,3]{1,0:T(8,128)}), f32[128,3]{1,0:T(8,128)}) %reduce-scatter.37.cloned.1.call-update) | async-done | bytes 1552
  1861.2 4.9 all-reduce.1
  1867.3 82.5 %all-reduce.20.cloned.1.call-done = (bf16[3,128,512]{2,1,0:T(8,128)(2,1)}, bf16[512,128]{1,0:T(8,128)(2,1)}, bf16[3,128,512]{2,1,0:T(8,128)(2,1)}, bf16[512,128]...) async-done(((bf16[3,128,512]{2,1,0:T(8,128)(2,1)}, bf16[512,128]{1,0:T(8,128)(2,1)}, bf16[3,128,512]{2,1,0:T(8,128)(2,1)}, ...) | async-done | bytes 3145744 | tf_op jit(solution)/shard_map/psum | solution.py:255
  (296 shorter events, 92.9 us)
Async XLA Ops:
  7.2 215.6 %copy-start = (bf16[256,1024]{1,0:T(8,128)(2,1)S(1)}, bf16[256,1024]{1,0:T(8,128)(2,1)}, u32[]{:S(2)}) copy-start(bf16[256,1024]{1,0:T(8,128)(2,1)} %param.14) | copy-start | bytes 1572868
  7.2 41.6 %copy-start.11 = (bf16[512,1024]{1,0:T(8,128)(2,1)S(1)}, bf16[512,1024]{1,0:T(8,128)(2,1)}, u32[]{:S(2)}) copy-start(bf16[512,1024]{1,0:T(8,128)(2,1)} %param.13) | copy-start | bytes 3145732
  7.2 66.3 %all-gather.9.cloned.1.call-start = ((), (), s32[]{:S(2)}) async-start(), calls=%async_computation.12 | async-start | bytes 3538944 | tf_op jit(solution)/shard_map/all_gather | solution.py:140
  7.9 88.5 %all-gather.13.cloned.1.call-start = ((), (), s32[]{:S(2)}) async-start(), calls=%async_computation.14 | async-start | bytes 1572864 | tf_op jit(solution)/shard_map/all_gather | solution.py:161
  48.8 33.0 %copy-start.57 = (f32[512]{0:T(512)}, f32[512]{0:T(512)S(1)}, u32[]{:S(2)}) copy-start(f32[512]{0:T(512)S(1)} %broadcast_multiply_fusion.8) | copy-start | bytes 6148
  49.3 32.6 %copy-start.63 = (f32[512]{0:T(512)}, f32[512]{0:T(512)S(1)}, u32[]{:S(2)}) copy-start(f32[512]{0:T(512)S(1)} %add_rsqrt_fusion.2) | copy-start | bytes 6148
  49.3 32.5 %copy-start.51 = (f32[1,1024]{1,0:T(1,128)}, f32[1,1024]{1,0:T(1,128)S(1)}, u32[]{:S(2)}) copy-start(f32[1,1024]{1,0:T(1,128)S(1)} %get-tuple-element.40) | copy-start | bytes 12292
  49.3 32.5 %copy-start.72 = (f32[1,1024]{1,0:T(1,128)}, f32[1,1024]{1,0:T(1,128)S(1)}, u32[]{:S(2)}) copy-start(f32[1,1024]{1,0:T(1,128)S(1)} %get-tuple-element.43) | copy-start | bytes 12292
  49.3 198.6 %copy-start.74 = (f32[1,1024]{1,0:T(1,128)}, f32[1,1024]{1,0:T(1,128)S(1)}, u32[]{:S(2)}) copy-start(f32[1,1024]{1,0:T(1,128)S(1)} %get-tuple-element.42) | copy-start | bytes 12292
  49.3 516.5 %copy-start.70 = (f32[1,1024]{1,0:T(1,128)}, f32[1,1024]{1,0:T(1,128)S(1)}, u32[]{:S(2)}) copy-start(f32[1,1024]{1,0:T(1,128)S(1)} %get-tuple-element.41) | copy-start | bytes 12292
  76.3 4.1 copy-start.69
  76.3 43.5 %all-gather.11.cloned.1.call-start = ((), (), s32[]{:S(2)}) async-start(), calls=%async_computation.13 | async-start | bytes 1572864 | tf_op jit(solution)/shard_map/all_gather | solution.py:162
  79.2 82.2 %all-gather.15.cloned.1.call-start = ((), (), s32[]{:S(2)}) async-start(), calls=%async_computation.15 | async-start | bytes 1179648 | tf_op jit(solution)/shard_map/all_gather | solution.py:141
  79.8 143.0 %all-gather.17.cloned.1.call-start = ((), (), s32[]{:S(2)}) async-start(), calls=%async_computation.17 | async-start | bytes 3538944 | tf_op jit(solution)/shard_map/all_gather | solution.py:142
  80.4 165.1 %all-reduce.10.cloned.1.call-start = ((), (), s32[]{:S(2)}) async-start(), calls=%async_computation.16 | async-start | bytes 4194304 | tf_op jit(solution)/shard_map/psum | solution.py:106
  84.0 37.3 %copy-start.24 = (bf16[512,512]{0,1:T(8,128)(2,1)}, bf16[512,512]{0,1:T(8,128)(2,1)S(1)}, u32[]{:S(2)}) copy-start(bf16[512,512]{0,1:T(8,128)(2,1)S(1)} %convolution_convert_fusion.4) | copy-start | bytes 1572868
  97.9 28.1 %copy-start.14 = (bf16[1024,512]{0,1:T(8,128)(2,1)}, bf16[1024,512]{0,1:T(8,128)(2,1)S(1)}, u32[]{:S(2)}) copy-start(bf16[1024,512]{0,1:T(8,128)(2,1)S(1)} %copy.49) | copy-start | bytes 3145732
  121.4 8.2 copy-start.23
  126.0 5.8 copy-start.1
  126.0 6.1 copy-start.47
  129.6 6.4 copy-start.49
  136.0 28.7 %copy-start.26 = (bf16[8,64,512]{2,1,0:T(8,128)(2,1)}, bf16[8,64,512]{2,1,0:T(8,128)(2,1)S(1)}, u32[]{:S(2)}) copy-start(bf16[8,64,512]{2,1,0:T(8,128)(2,1)S(1)} %fusion.44) | copy-start | bytes 1572868
  161.3 4.1 copy-start.76
  164.7 123.8 %all-gather.19.cloned.1.call-start = ((), (), s32[]{:S(2)}) async-start(), calls=%async_computation.18 | async-start | bytes 1179648 | tf_op jit(solution)/shard_map/all_gather | solution.py:143
  165.4 146.6 %all-reduce.12.cloned.1.call-start = ((), (), s32[]{:S(2)}) async-start(), calls=%async_computation.19 | async-start | bytes 4194304 | tf_op jit(solution)/shard_map/psum | solution.py:106
  232.6 17.7 copy-start.19
  247.6 410.2 %copy-start.53 = (f32[512]{0:T(512)}, f32[512]{0:T(512)S(1)}, u32[]{:S(2)}) copy-start(f32[512]{0:T(512)S(1)} %broadcast_multiply_fusion.7) | copy-start | bytes 6148
  248.0 409.9 %copy-start.59 = (f32[512]{0:T(512)}, f32[512]{0:T(512)S(1)}, u32[]{:S(2)}) copy-start(f32[512]{0:T(512)S(1)} %add_rsqrt_fusion.1) | copy-start | bytes 6148
  256.8 35.0 %copy-start.28 = (bf16[8,64,512]{2,1,0:T(8,128)(2,1)}, bf16[8,64,512]{2,1,0:T(8,128)(2,1)S(1)}, u32[]{:S(2)}) copy-start(bf16[8,64,512]{2,1,0:T(8,128)(2,1)S(1)} %fusion.38) | copy-start | bytes 1572868
  291.8 148.9 %all-gather.23.cloned.1.call-start = ((), (), s32[]{:S(2)}) async-start(), calls=%async_computation.21 | async-start | bytes 9437184 | tf_op jit(solution)/shard_map/all_gather | solution.py:145
  292.5 273.3 %all-gather.21.cloned.1.call-start = ((), (), s32[]{:S(2)}) async-start(), calls=%async_computation.20 | async-start | bytes 9437184 | tf_op jit(solution)/shard_map/all_gather | solution.py:144
  293.1 318.6 %all-reduce.14.cloned.1.call-start = ((), (), s32[]{:S(2)}) async-start(), calls=%async_computation.22 | async-start | bytes 4194304 | tf_op jit(solution)/shard_map/psum | solution.py:110
  314.0 301.6 %copy-start.55 = (f32[512]{0:T(512)}, f32[512]{0:T(512)S(1)}, u32[]{:S(2)}) copy-start(f32[512]{0:T(512)S(1)} %broadcast_multiply_fusion.6) | copy-start | bytes 6148
  315.6 299.9 %copy-start.61 = (f32[512]{0:T(512)}, f32[512]{0:T(512)S(1)}, u32[]{:S(2)}) copy-start(f32[512]{0:T(512)S(1)} %add_rsqrt_fusion) | copy-start | bytes 6148
  565.8 20.5 %copy-start.77 = (bf16[1024,4096]{1,0:T(8,128)(2,1)S(1)}, bf16[1024,4096]{1,0:T(8,128)(2,1)}, u32[]{:S(2)}) copy-start(bf16[1024,4096]{1,0:T(8,128)(2,1)} %all-gather.21.cloned.1.call-done) | copy-start | bytes 25165828
  592.2 62.4 %all-reduce.16.cloned.1.call-start = ((), (), s32[]{:S(2)}) async-start(), calls=%async_computation.23 | async-start | bytes 4194304 | tf_op jit(solution)/shard_map/psum | solution.py:110
  611.7 8.6 slice-start.4
  615.6 4.8 slice-start.5
  632.0 4.7 copy-start.48
  632.0 4.7 copy-start.50
  632.1 79.0 %reduce-scatter.21.cloned.1.call-start = ((), (), s32[]{:S(2)}) async-start(), calls=%async_computation.26 | async-start | bytes 786432 | tf_op jit(solution)/shard_map/reduce_scatter | solution.py:212
  636.7 77.2 %reduce-scatter.23.cloned.1.call-start = ((), (), s32[]{:S(2)}) async-start(), calls=%async_computation.27 | async-start | bytes 786432 | tf_op jit(solution)/shard_map/reduce_scatter | solution.py:215
  643.1 84.2 %reduce-scatter.17.cloned.1.call-start = ((), (), s32[]{:S(2)}) async-start(), calls=%async_computation.24 | async-start | bytes 1572864 | tf_op jit(solution)/shard_map/reduce_scatter | solution.py:206
  661.5 15.0 slice-start
  661.5 15.0 slice-start.1
  661.5 15.9 slice-start.2
  661.5 17.1 slice-start.3
  678.6 7.9 copy-start.25
  686.5 3.7 copy-start.18
  690.2 45.3 %reduce-scatter.19.cloned.1.call-start = ((), (), s32[]{:S(2)}) async-start(), calls=%async_computation.25 | async-start | bytes 1572864 | tf_op jit(solution)/shard_map/reduce_scatter | solution.py:209
  698.8 95.8 %all-reduce.18.cloned.1.call-start = ((), (), s32[]{:S(2)}) async-start(), calls=%async_computation.36 | async-start | bytes 10485760 | tf_op jit(solution)/shard_map/psum | solution.py:106
  740.3 103.6 %reduce-scatter.31.cloned.1.call-start = ((), (), s32[]{:S(2)}) async-start(), calls=%async_computation.31 | async-start | bytes 2359296 | tf_op jit(solution)/shard_map/reduce_scatter | solution.py:248
  745.0 170.7 %reduce-scatter.27.cloned.1.call-start = ((), (), s32[]{:S(2)}) async-start(), calls=%async_computation.29 | async-start | bytes 2359296 | tf_op jit(solution)/shard_map/reduce_scatter | solution.py:246
  750.1 286.9 %reduce-scatter.29.cloned.1.call-start = ((), (), s32[]{:S(2)}) async-start(), calls=%async_computation.30 | async-start | bytes 7077888 | tf_op jit(solution)/shard_map/reduce_scatter | solution.py:247
  757.0 401.6 %reduce-scatter.25.cloned.1.call-start = ((), (), s32[]{:S(2)}) async-start(), calls=%async_computation.28 | async-start | bytes 7077888 | tf_op jit(solution)/shard_map/reduce_scatter | solution.py:245
  765.0 679.8 %reduce-scatter.35.cloned.1.call-start = ((), (), s32[]{:S(2)}) async-start(), calls=%async_computation.33 | async-start | bytes 18874368 | tf_op jit(solution)/shard_map/reduce_scatter | solution.py:250
  782.2 948.1 %reduce-scatter.33.cloned.1.call-start = ((), (), s32[]{:S(2)}) async-start(), calls=%async_computation.32 | async-start | bytes 18874368 | tf_op jit(solution)/shard_map/reduce_scatter | solution.py:249
  794.6 1000.9 %reduce-scatter.39.cloned.1.call-start = ((), (), s32[]{:S(2)}) async-start(), calls=%async_computation.35 | async-start | bytes 589824
  794.6 4.0 copy-start.65
  794.7 4.0 copy-start.67
  798.6 1061.7 %reduce-scatter.37.cloned.1.call-start = ((), (), s32[]{:S(2)}) async-start(), calls=%async_computation.34 | async-start | bytes 589824
  799.8 1150.1 %all-reduce.20.cloned.1.call-start = ((), (), s32[]{:S(2)}) async-start(), calls=%async_computation.37 | async-start | bytes 6291456 | tf_op jit(solution)/shard_map/psum | solution.py:255
  1949.8 5.3 copy-start.46
  1949.8 6.3 copy-start.38
  (47 other events, 92.1 us)
Sparse Core Ops, SparseCore 0:
  10.2 63.2 all-gather.8
  76.4 19.9 all-gather.12
  98.5 21.2 all-gather.10
  121.8 39.5 all-gather.14
  163.4 59.3 all-gather.16
  225.6 19.8 all-reduce.9
  247.7 40.7 all-gather.18
  291.9 20.0 all-reduce.11
  314.1 126.5 all-gather.22
  442.7 123.1 all-gather.20
  592.3 19.3 all-reduce.13
  632.2 22.3 all-reduce.15
  657.4 15.7 reduce-scatter.20
  675.3 14.5 reduce-scatter.22
  692.6 20.3 reduce-scatter.16
  715.1 20.2 reduce-scatter.18
  740.4 30.3 all-reduce.17
  774.6 69.2 reduce-scatter.30
  848.5 67.1 reduce-scatter.26
  919.6 117.3 reduce-scatter.28
  1041.1 117.5 reduce-scatter.24
  1162.9 281.8 reduce-scatter.34
  1448.5 281.7 reduce-scatter.32
  1734.5 60.9 reduce-scatter.38
  1799.4 60.8 reduce-scatter.36
  1864.2 85.6 all-reduce.19
where the time goes:
time: 1980 us; the launch traced here: 1970 us
  waiting for transfers between devices  1600 us (81%)
  matrix products  189 us (10%)
  other arithmetic  73.1 us (4%)
  blocking collectives  59.4 us (3%)
  local copies, waits for them, and re-layouts  32.7 us (2%)
    reduce_scatter x1, waiting for transfers between devices, per_device(): lax.psum_scatter(grad_down, 'dp', scatter_dimension=1, tiled=True)  284 us
    reduce_scatter x1, waiting for transfers between devices, per_device(): lax.psum_scatter(grad_ffn, 'dp', scatter_dimension=0, tiled=True)  283 us
    all_gather x1, waiting for transfers between devices, per_device(): lax.all_gather(ffn_out, 'dp', axis=1, tiled=True)  125 us
    unnamed x28, waiting for transfers between devices  125 us
    reduce_scatter x1, waiting for transfers between devices, per_device(): lax.psum_scatter(grad_cross_in, 'dp', scatter_dimension=1, tiled=True)  120 us
    reduce_scatter x1, waiting for transfers between devices, per_device(): lax.psum_scatter(grad_self_in, 'dp', scatter_dimension=1, tiled=True)  120 us
    all_gather x1, waiting for transfers between devices, per_device(): lax.all_gather(ffn_in, 'dp', axis=0, tiled=True)  114 us
    psum x1, waiting for transfers between devices, per_device(): lax.psum(shards[0].astype(jnp.bfloat16), 'ctx').astype(jnp.float32)  82.5 us
  transfers between devices with their start and end apart: 26, of which 22 were waited for; matrix products, arithmetic and copies ran while one was open for 11% of the time, Pallas kernels for 0%

commit v1 on v0

v1 whole, which is shorter than its diff:
```python
import functools

import jax
import jax.numpy as jnp
import numpy as np
from jax import lax
from jax.experimental import pallas as pl
from jax.experimental.pallas import tpu as pltpu
from jax.sharding import PartitionSpec as P

HEAD_DIM = 64
SCALE = HEAD_DIM**-0.5
EPSILON = 1e-05
MASKED = -1000000000.0
RING_MOST = 8

f32 = jnp.float32
bf16 = jnp.bfloat16
hold = lax.optimization_barrier


def product(left, right):
    return jnp.dot(left, right, preferred_element_type=f32)


def left_product(left, right):
    return lax.dot_general(left, right, (((0,), (0,)), ((), ())), preferred_element_type=f32)


def right_product(left, right):
    return lax.dot_general(left, right, (((1,), (1,)), ((), ())), preferred_element_type=f32)


def norm_forward(values, gain, shift):
    centre = jnp.mean(values, axis=-1, keepdims=True)
    centred = values - centre
    factor = lax.rsqrt(jnp.mean(centred * centred, axis=-1, keepdims=True) + EPSILON)
    normal = centred * factor
    return normal * gain + shift, normal, factor


def norm_backward(grad_norm, normal, factor, gain):
    scaled = grad_norm * gain
    inner = (
        scaled
        - jnp.mean(scaled, axis=-1, keepdims=True)
        - normal * jnp.mean(scaled * normal, axis=-1, keepdims=True)
    )
    return factor * inner


def norm_sums(grad_norm, normal):
    return jnp.stack([jnp.sum(grad_norm * normal, axis=0), jnp.sum(grad_norm, axis=0)])


def split_heads(values):
    return values.reshape(values.shape[0], values.shape[1] // HEAD_DIM, HEAD_DIM)


def masked_scores(queries, keys, allowed):
    scores = jnp.einsum(
        "qhd,khd->hqk", split_heads(queries), split_heads(keys), preferred_element_type=f32
    )
    return jnp.where(allowed[None], scores * SCALE, MASKED)


def attend_forward(queries, keys, values, allowed):
    scores = masked_scores(queries, keys, allowed)
    peak = jnp.max(scores, axis=-1, keepdims=True)
    expo = jnp.exp(scores - peak)
    total = jnp.sum(expo, axis=-1, keepdims=True)
    probs = (expo / total).astype(bf16)
    mixed = jnp.einsum("hqk,khd->qhd", probs, split_heads(values), preferred_element_type=f32)
    return mixed.reshape(queries.shape).astype(bf16), peak + jnp.log(total)


def attend_backward(grad_mixed, queries, keys, values, allowed, log_total):
    scores = masked_scores(queries, keys, allowed)
    probs = jnp.exp(scores - log_total)
    grad_heads = split_heads(grad_mixed)
    grad_values = jnp.einsum(
        "hqk,qhd->khd", probs.astype(bf16), grad_heads, preferred_element_type=f32
    )
    grad_probs = jnp.einsum(
        "qhd,khd->hqk", grad_heads, split_heads(values), preferred_element_type=f32
    )
    grad_scores = probs * (grad_probs - jnp.sum(probs * grad_probs, axis=-1, keepdims=True))
    grad_scores = grad_scores.astype(bf16)
    grad_queries = jnp.einsum(
        "hqk,khd->qhd", grad_scores, split_heads(keys), preferred_element_type=f32
    )
    grad_keys = jnp.einsum(
        "hqk,qhd->khd", grad_scores, split_heads(queries), preferred_element_type=f32
    )
    return (
        (grad_queries * SCALE).reshape(queries.shape).astype(bf16),
        (grad_keys * SCALE).reshape(keys.shape).astype(bf16),
        grad_values.reshape(values.shape).astype(bf16),
    )


def gelu_tanh(values):
    return jax.nn.gelu(values, approximate=True)


def move_blocks(array, places):
    rows, columns = array.shape
    count = places.shape[0]
    width = columns // count

    def body(places_ref, in_ref, out_ref):
        out_ref[...] = in_ref[...]

    return pl.pallas_call(
        body,
        grid_spec=pltpu.PrefetchScalarGridSpec(
            num_scalar_prefetch=1,
            grid=(count,),
            in_specs=[pl.BlockSpec((rows, width), lambda k, places_ref: (0, places_ref[k]))],
            out_specs=pl.BlockSpec((rows, width), lambda k, places_ref: (0, k)),
        ),
        out_shape=jax.ShapeDtypeStruct(array.shape, array.dtype),
    )(places, array)


def swap(values, axis):
    return lax.ppermute(values, axis, [(0, 1), (1, 0)])


class Ring:
    def __init__(self, size):
        self.size = size
        self.short = size <= RING_MOST and size % 2 == 0
        half = size // 2
        if self.short:
            self.order = [2 * p if p < half else 2 * (size - 1 - p) + 1 for p in range(size)]
        else:
            self.order = list(range(size))
        position = np.zeros(size, np.int32)
        position[self.order] = np.arange(size)
        there = np.zeros((size, size), np.int32)
        back = np.zeros((size, size), np.int32)
        for device in range(size):
            for k in range(size):
                place = self.order[(position[device] + k) % size] if self.short else k
                there[device, k] = place
                back[device, place] = k
        self.there, self.back = there, back

    def places(self, table):
        return lax.dynamic_index_in_dim(jnp.asarray(table), lax.axis_index("dp"), 0, False)

    def into(self, array):
        return move_blocks(array, self.places(self.there)) if self.short else array

    def out_of(self, array):
        return move_blocks(array, self.places(self.back)) if self.short else array

    def send(self, values, step):
        size, order = self.size, self.order
        pairs = [(order[p], order[(p + step) % size]) for p in range(size)]
        return lax.ppermute(values, "dp", pairs)

    def gather(self, shard):
        if not self.short:
            return lax.all_gather(shard, "dp", axis=1, tiled=True)
        size = self.size
        cut = shard.shape[-1] // 2
        ahead = behind = shard
        from_ahead, from_behind = [], []
        for _ in range(size // 2 - 1):
            ahead = self.send(ahead, -1)
            behind = self.send(behind, 1)
            from_ahead.append(ahead)
            from_behind.append(behind)
        far = [self.send(ahead[..., :cut], -1), self.send(behind[..., cut:], 1)]
        middle = jnp.concatenate(far, -1)
        return jnp.concatenate([shard] + from_ahead + [middle] + from_behind[::-1], 1)

    def scatter(self, full):
        size = self.size
        if not self.short:
            return lax.psum_scatter(full.astype(bf16), "dp", scatter_dimension=1, tiled=True).astype(f32)
        rows = full.shape[1] // size
        half = size // 2
        blocks = [full[:, k * rows : (k + 1) * rows].astype(f32) for k in range(size)]
        cut = full.shape[-1] // 2
        ahead = self.send(blocks[half][..., :cut].astype(bf16), 1)
        behind = self.send(blocks[half][..., cut:].astype(bf16), -1)
        for k in range(half - 1, 0, -1):
            up, down = blocks[k], blocks[size - k]
            if k == half - 1:
                up = jnp.concatenate([up[..., :cut] + ahead.astype(f32), up[..., cut:]], -1)
                down = jnp.concatenate([down[..., :cut], down[..., cut:] + behind.astype(f32)], -1)
            else:
                up = up + ahead.astype(f32)
                down = down + behind.astype(f32)
            ahead = self.send(up.astype(bf16), 1)
            behind = self.send(down.astype(bf16), -1)
        return blocks[0] + (ahead.astype(f32) + behind.astype(f32))

    def scatter_few(self, full):
        size = self.size
        if not self.short:
            return lax.psum_scatter(full, "dp", scatter_dimension=1, tiled=True)
        width = full.shape[1] // size
        blocks = [full[:, k * width : (k + 1) * width] for k in range(size)]
        parts = [blocks[0]] + [self.send(blocks[k], k) for k in range(1, size)]
        return sum(parts[1:], parts[0])


def per_device(
    ring,
    hidden_in,
    encoder_states,
    out_grad,
    target_ids,
    source_ids,
    self_in,
    self_out,
    cross_in,
    cross_out,
    ffn_in,
    ffn_out,
    norm_gain,
    norm_bias,
):
    ctx = lax.axis_index("ctx")
    core = lax.axis_index("tp")
    rows = hidden_in.shape[0]
    source_rows = encoder_states.shape[0]

    def own_half(array, axis, place=ctx):
        half = array.shape[axis] // 2
        return lax.dynamic_slice_in_dim(array, place * half, half, axis)

    def both_rows(own):
        part = own_half(own, 0, core)
        got = swap(part, "ctx")
        rest = swap(got, "tp")
        low = jnp.where(core == 0, got, rest)
        high = jnp.where(core == 0, rest, got)
        return jnp.concatenate([own, low, high], 0)

    def turned(values):
        half = values.shape[0] // 2
        return jnp.concatenate([values[half:], values[:half]], 0)

    def core_sum(partial):
        part = hold(partial.astype(bf16))
        return part.astype(f32) + swap(part, "tp").astype(f32)

    def row_sum(partial):
        count = partial.shape[0] // 2
        low = hold(partial.astype(bf16))
        mine, theirs = low[:count], low[count:]
        keep = own_half(theirs, 0, core)
        give = own_half(theirs, 0, 1 - core)
        summed = (keep.astype(f32) + swap(give, "tp").astype(f32)).astype(bf16)
        got = swap(summed, "ctx")
        rest = swap(got, "tp")
        far = jnp.concatenate([jnp.where(core == 0, got, rest), jnp.where(core == 0, rest, got)], 0)
        near = mine.astype(f32) + swap(mine, "tp").astype(f32)
        return near + far.astype(f32)

    def both_columns(part):
        part = hold(part.astype(bf16))
        other = swap(part, "ctx")
        low = jnp.where(ctx == 0, part, other)
        high = jnp.where(ctx == 0, other, part)
        return jnp.concatenate([low, high], -1).astype(f32)

    first_shard = own_half(self_in, 2)
    cross_half = own_half(cross_in, 2)
    out_halves = jnp.stack([own_half(self_out, 0).T, own_half(cross_out, 0).T])
    key_shard = cross_half[1:]
    third_shard = jnp.concatenate([out_halves[:1], cross_half[:1], out_halves[1:]], 0)
    up_shard = own_half(ffn_in, 1)[None]
    down_shard = own_half(ffn_out, 0).T[None]

    vectors = jnp.concatenate([norm_gain, norm_bias], 0)
    vectors = lax.all_gather(vectors, "dp", axis=1, tiled=True).astype(f32)
    vectors = jnp.concatenate([vectors, jnp.zeros((2, vectors.shape[1]), f32)], 0)
    vectors = ring.into(vectors)
    gains, biases = vectors[0:3, None, :], vectors[3:6, None, :]

    hidden = both_rows(ring.into(hidden_in))
    first_w = ring.gather(first_shard)
    key_shard, first_w = hold((key_shard, first_w))
    third_shard, key_shard = hold((third_shard, key_shard))
    third_w = ring.gather(third_shard)
    key_w = ring.gather(key_shard)
    third_w = jnp.concatenate([third_w, swap(third_w, "ctx")], -1)
    up_shard, down_shard, third_w = hold((up_shard, down_shard, third_w))
    up_w = ring.gather(up_shard)[0]
    down_w = ring.gather(down_shard)[0]
    source = both_rows(ring.into(encoder_states))
    out_cot = both_rows(ring.into(out_grad))

    def both_order(vector):
        half = vector.shape[0] // 2
        return jnp.concatenate(
            [
                lax.dynamic_slice_in_dim(vector, ctx * half, half),
                lax.dynamic_slice_in_dim(vector, (1 - ctx) * half, half),
            ]
        )

    target_row = both_order(target_ids[0])
    source_row = both_order(source_ids[0])
    place = both_order(jnp.arange(2 * rows, dtype=jnp.int32))
    self_allowed = (target_row[:, None] == target_row[None, :]) & (place[None, :] <= place[:, None])
    cross_allowed = target_row[:rows, None] == source_row[None, :]

    start_rows = hidden.astype(f32)
    normed, normal_one, factor_one = norm_forward(start_rows, gains[0], biases[0])
    input_one = normed.astype(bf16)
    queries = product(input_one, first_w[0]).astype(bf16)
    keys = product(input_one, first_w[1]).astype(bf16)
    values = product(input_one, first_w[2]).astype(bf16)
    mixed, total_one = attend_forward(queries, keys, values, self_allowed)
    mixed_one = jnp.concatenate([mixed[:rows], swap(mixed[rows:], "ctx")], 1)
    self_o, cross_q, cross_o = third_w[0], third_w[1], third_w[2]
    first_rows = start_rows[:rows] + core_sum(right_product(mixed_one, self_o))

    key_cross = product(source, key_w[0]).astype(bf16)
    value_cross = product(source, key_w[1]).astype(bf16)
    pair = jnp.concatenate([key_cross, value_cross], 1)
    other = swap(turned(pair), "ctx")
    width = key_cross.shape[1]
    key_cross = jnp.concatenate([key_cross, other[:, :width]], 1)
    value_cross = jnp.concatenate([value_cross, other[:, width:]], 1)
    normed, normal_two, factor_two = norm_forward(first_rows, gains[1], biases[1])
    input_two = normed.astype(bf16)
    cross_queries = product(input_two, cross_q).astype(bf16)
    mixed_two, total_two = attend_forward(cross_queries, key_cross, value_cross, cross_allowed)
    second_rows = first_rows + core_sum(right_product(mixed_two, cross_o))

    normed, normal_three, factor_three = norm_forward(second_rows, gains[2], biases[2])
    input_three = both_rows(normed.astype(bf16))
    activated, gelu_pull = jax.vjp(gelu_tanh, product(input_three, up_w))
    activated = activated.astype(bf16)
    grad_up = gelu_pull(product(out_cot, down_w))[0].astype(bf16)
    grad_norm = row_sum(right_product(grad_up, up_w))
    result = (second_rows + row_sum(right_product(activated, down_w))).astype(bf16)
    grad_up_w = left_product(input_three, grad_up)
    grad_down_w = left_product(out_cot, activated)
    up_sum = ring.scatter(grad_up_w[None])
    down_sum = ring.scatter(grad_down_w[None])

    grad_rows = out_cot[:rows].astype(f32)
    sums_three = norm_sums(grad_norm, normal_three)
    grad_second = grad_rows + norm_backward(grad_norm, normal_three, factor_three, gains[2])

    grad_branch = grad_second.astype(bf16)
    grad_cross_o = left_product(grad_branch, mixed_two)
    grad_mixed = product(grad_branch, cross_o).astype(bf16)
    grad_cq, grad_ck, grad_cv = attend_backward(
        grad_mixed, cross_queries, key_cross, value_cross, cross_allowed, total_two
    )
    grad_norm = core_sum(right_product(grad_cq, cross_q))
    grad_cross_q = left_product(input_two, grad_cq)
    given = swap(turned(jnp.concatenate([grad_ck[:, width:], grad_cv[:, width:]], 1)), "ctx")
    grad_ck = (grad_ck[:, :width].astype(f32) + given[:, :width].astype(f32)).astype(bf16)
    grad_cv = (grad_cv[:, :width].astype(f32) + given[:, width:].astype(f32)).astype(bf16)
    grad_key_w = jnp.stack([left_product(source, grad_ck), left_product(source, grad_cv)])
    grad_source = row_sum(right_product(grad_ck, key_w[0]) + right_product(grad_cv, key_w[1]))

    sums_two = norm_sums(grad_norm, normal_two)
    grad_first = grad_second + norm_backward(grad_norm, normal_two, factor_two, gains[1])

    grad_branch = grad_first.astype(bf16)
    grad_self_o = left_product(grad_branch, mixed_one)
    grad_mixed = product(grad_branch, self_o).astype(bf16)
    head_width = mixed.shape[1]
    grad_mixed = jnp.concatenate(
        [grad_mixed[:, :head_width], swap(grad_mixed[:, head_width:], "ctx")], 0
    )
    grad_q, grad_k, grad_v = attend_backward(
        grad_mixed, queries, keys, values, self_allowed, total_one
    )
    grad_first_w = jnp.stack(
        [left_product(input_one, grad_q), left_product(input_one, grad_k), left_product(input_one, grad_v)]
    )
    first_sum = ring.scatter(grad_first_w)
    partial = (
        right_product(grad_q, first_w[0])
        + right_product(grad_k, first_w[1])
        + right_product(grad_v, first_w[2])
    )
    sums_one = norm_sums(partial, normal_one)
    grad_norm = row_sum(partial)
    grad_input = grad_first + norm_backward(
        grad_norm, normal_one[:rows], factor_one[:rows], gains[0]
    )

    third = jnp.stack([grad_self_o, grad_cross_q, grad_cross_o])
    cut = third.shape[2] // 2
    third = third[..., :cut] + swap(third[..., cut:].astype(bf16), "ctx").astype(f32)
    third_sum = ring.scatter(third)
    key_sum = ring.scatter(grad_key_w)

    sums_one = sums_one + swap(sums_one, "tp")
    sums = jnp.concatenate([sums_one, sums_two, sums_three, jnp.zeros_like(sums_one)], 0)
    sums = ring.scatter_few(sums + swap(sums, "ctx"))
    grad_gains = jnp.stack([sums[0], sums[2], sums[4]])
    grad_biases = jnp.stack([sums[1], sums[3], sums[5]])

    first_out = both_columns(first_sum)
    third_out = both_columns(third_sum)
    key_out = both_columns(key_sum)
    return (
        ring.out_of(result),
        ring.out_of(grad_input),
        ring.out_of(grad_source),
        first_out,
        third_out[0].T,
        jnp.concatenate([third_out[1:2], key_out], 0),
        third_out[2].T,
        both_columns(up_sum)[0],
        both_columns(down_sum)[0].T,
        grad_gains,
        grad_biases,
    )


def solution(mesh):
    return jax.shard_map(
        functools.partial(per_device, Ring(mesh.shape["dp"])),
        mesh=mesh,
        in_specs=(
            P(("dp", "ctx"), None),
            P(("dp", "ctx"), None),
            P(("dp", "ctx"), None),
            P("dp", None),
            P("dp", None),
            P(None, "dp", "tp"),
            P("tp", "dp"),
            P(None, "dp", "tp"),
            P("tp", "dp"),
            P("dp", "tp"),
            P("tp", "dp"),
            P(None, "dp"),
            P(None, "dp"),
        ),
        out_specs=(
            P(("dp", "ctx"), None),
            P(("dp", "ctx"), None),
            P(("dp", "ctx"), None),
            P(None, "dp", "tp"),
            P("tp", "dp"),
            P(None, "dp", "tp"),
            P("tp", "dp"),
            P("dp", "tp"),
            P("tp", "dp"),
            P(None, "dp"),
            P(None, "dp"),
        ),
        check_vma=False,
    )
```

time: 1980 us -> 733 us (0.37)
  waiting for transfers between devices: 1600 us -> 233 us
  starting transfers between devices: 1.52 us -> 124 us
  matrix products: 189 us -> 146 us
  Pallas kernels: 0 us -> 40.4 us
  blocking collectives: 59.4 us -> 26.3 us
  local copies, waits for them, and re-layouts: 32.7 us -> 60.8 us
    reduce_scatter x10 -> x0, waiting for transfers between devices: 926 us -> none  [the longest x1 284 us: per_device(): lax.psum_scatter(grad_down, 'dp', scatter_dimension=1, tiled=True)]
    all_gather x8 -> x0, waiting for transfers between devices: 411 us -> none  [the longest x1 125 us: per_device(): lax.all_gather(ffn_out, 'dp', axis=1, tiled=True)]
    ppermute x0 -> x127, waiting for transfers between devices: none -> 233 us  [the longest x87 144 us: send(): return lax.ppermute(values, 'dp', pairs)]
    psum x6 -> x0, waiting for transfers between devices: 135 us -> none  [the longest x1 82.5 us: per_device(): lax.psum(shards[0].astype(jnp.bfloat16), 'ctx').astype(jnp.float32)]
    unnamed x28 -> x0, waiting for transfers between devices: 125 us -> none
    ppermute x0 -> x127, starting transfers between devices: none -> 124 us  [the longest x87 99.7 us: send(): return lax.ppermute(values, 'dp', pairs)]
    pallas_call x0 -> x7, Pallas kernels: none -> 40.4 us  [move_blocks(): pl.pallas_call(body, grid_spec=pltpu.PrefetchScalarGridSpec(num_scalar_pr...]
    all_gather x4 -> x1, blocking collectives: 54.5 us -> 26.3 us  [per_device(): vectors = lax.all_gather(vectors, 'dp', axis=1, tiled=True).astype(f32)]
  transfers between devices with their start and end apart: 26 -> 127, of which waited for: 22 -> 55; matrix products, arithmetic and copies ran while one was open for 11% -> 31% of each run, Pallas kernels for 0% -> 6%
where the time goes in v1:
time: 733 us; the launch traced here: 727 us
  waiting for transfers between devices  233 us (32%)
  matrix products  146 us (20%)
  starting transfers between devices  124 us (17%)
  other arithmetic  92.8 us (13%)
  local copies, waits for them, and re-layouts  60.8 us (8%)
  Pallas kernels  40.4 us (6%)
  blocking collectives  26.3 us (4%)
    ppermute x87, waiting for transfers between devices, send(): return lax.ppermute(values, 'dp', pairs)  144 us
    ppermute x87, starting transfers between devices, send(): return lax.ppermute(values, 'dp', pairs)  99.7 us
    ppermute x40, waiting for transfers between devices, swap(): return lax.ppermute(values, axis, [(0, 1), (1, 0)])  89.6 us
    pallas_call x7, Pallas kernels, move_blocks(): pl.pallas_call(body, grid_spec=pltpu.PrefetchScalarGridSpec(num_scalar_pr...  40.4 us
    unnamed x240, local copies, waits for them, and re-layouts  32.3 us
    dot_general x10, matrix products, product(): return jnp.dot(left, right, preferred_element_type=f32)  32.3 us
    dot_general x10, matrix products, left_product(): lax.dot_general(left, right, (((0,), (0,)), ((), ())), preferred_element_...  31.3 us
    dot_general x10, matrix products, right_product(): lax.dot_general(left, right, (((1,), (1,)), ((), ())), preferred_element_...  30.7 us
  transfers between devices with their start and end apart: 127, of which 55 were waited for; matrix products, arithmetic and copies ran while one was open for 31% of the time, Pallas kernels for 6%

profile of v1, /device:TPU:0, one launch (start us, length us, event | category | flops | bytes accessed | tf_op | source)
XLA Modules:
  0.0 726.7 jit_solution(13062916962331675568)
XLA Ops:
  2.5 3.0 collective-permute-start.6
  6.7 5.4 shard_map.232
  15.7 6.0 shard_map.230
  23.7 6.0 shard_map.234
  33.5 26.3 %all_gather.3 = bf16[6,1024]{1,0:T(8,128)(2,1)S(1)} all-gather(bf16[6,128]{1,0:T(8,128)(2,1)S(1)} %pad_maximum_fusion.33), channel_id=1, replica_groups=mesh['dp'=8,'ctx'=2,'tp'=2] {'dp'}, dimensions={1}, use_global_device_ids=true | all-gather | bytes 13824 | tf_op jit(solution)/shard_map/all_gather | solution.py:282
  64.7 4.6 shard_map.231
  120.4 7.4 %fusion.173 = (f32[4,1024]{1,0:T(4,128)S(1)}, f32[4,1024,1024]{1,2,0:T(8,128)}) fusion(bf16[1024,4,64]{0,2,1:T(8,128)(2,1)S(1)} %bitcast.215, bf16[1024,4,64]{0,2,1:T(8,128)(2,1)S(1)} %bitcast.213, pred[1024,1024]{0,1:T(8,128)(4,1)S(1)} %compare_and_fusion), kind=kOutput, calls=%fused_computation.431 | convolution fusion | flops 549449728 | bytes 18890752 | tf_op jit(solution)/shard_map/qhd,khd->hqk/dot_general | solution.py:61
  127.8 8.0 %fusion = f32[4,1024]{1,0:T(4,128)S(1)} fusion(f32[4,1024,1024]{1,2,0:T(8,128)} %get-tuple-element.180, f32[4,1024]{1,0:T(4,128)S(1)} %get-tuple-element.179), kind=kLoop, calls=%fused_computation.6 | loop fusion | flops 8384512 | bytes 16809984 | tf_op jit(solution)/shard_map/reduce_sum | solution.py:71
  135.8 9.0 %fusion.51 = bf16[1024,4,64]{0,2,1:T(8,128)(2,1)S(1)} fusion(bf16[1024,4,64]{0,2,1:T(8,128)(2,1)} %bitcast.229, f32[4,1024,1024]{1,2,0:T(8,128)} %get-tuple-element.180, f32[4,1024]{1,0:T(4,128)S(1)} %fusion, f32[4,1024]{1,0:T(4,128)S(1)} %get-tuple-element.179), kind=kOutput, calls=%fused_computation.130 | convolution fusion | flops 549715968 | bytes 17858560 | tf_op jit(solution)/shard_map/hqk,khd->qhd/dot_general | solution.py:73
  158.1 2.3 collective-permute-done.18
  170.5 39.2 %collective-permute-done.31 = bf16[512,512]{0,1:T(8,128)(2,1)S(1)} collective-permute-done((bf16[512,512]{0,1:T(8,128)(2,1)S(1)}, bf16[512,512]{0,1:T(8,128)(2,1)S(1)}, u32[]{:S(2)}, u32[]{:S(2)}) %collective-permute-start.31) | collective-permute-done | bytes 524320 | tf_op jit(solution)/shard_map/ppermute | solution.py:127
  215.3 9.1 %collective-permute-done.39 = bf16[1,128,2048]{2,1,0:T(8,128)(2,1)S(1)} collective-permute-done((bf16[1,128,2048]{2,1,0:T(8,128)(2,1)S(1)}, bf16[1,128,2048]{2,1,0:T(8,128)(2,1)S(1)}, u32[]{:S(2)}, u32[]{:S(2)}) %collective-permute-start.39) | collective-permute-done | bytes 524320 | tf_op jit(solution)/shard_map/ppermute | solution.py:162
  226.4 9.2 %collective-permute-done.47 = bf16[1,128,2048]{1,2,0:T(8,128)(2,1)S(1)} collective-permute-done((bf16[1,128,2048]{1,2,0:T(8,128)(2,1)S(1)}, bf16[1,128,2048]{1,2,0:T(8,128)(2,1)S(1)}, u32[]{:S(2)}, u32[]{:S(2)}) %collective-permute-start.47) | collective-permute-done | bytes 524320 | tf_op jit(solution)/shard_map/ppermute | solution.py:162
  238.1 8.8 %collective-permute-done.40 = bf16[1,128,2048]{2,1,0:T(8,128)(2,1)S(1)} collective-permute-done((bf16[1,128,2048]{2,1,0:T(8,128)(2,1)S(1)}, bf16[1,128,2048]{2,1,0:T(8,128)(2,1)S(1)}, u32[]{:S(2)}, u32[]{:S(2)}) %collective-permute-start.40) | collective-permute-done | bytes 524320 | tf_op jit(solution)/shard_map/ppermute | solution.py:162
  248.9 9.2 %collective-permute-done.48 = bf16[1,128,2048]{1,2,0:T(8,128)(2,1)S(1)} collective-permute-done((bf16[1,128,2048]{1,2,0:T(8,128)(2,1)S(1)}, bf16[1,128,2048]{1,2,0:T(8,128)(2,1)S(1)}, u32[]{:S(2)}, u32[]{:S(2)}) %collective-permute-start.48) | collective-permute-done | bytes 524320 | tf_op jit(solution)/shard_map/ppermute | solution.py:162
  269.7 3.7 collective-permute-done.49
  284.7 7.4 %collective-permute-done.33 = bf16[256,1024]{1,0:T(8,128)(2,1)S(1)} collective-permute-done((bf16[256,1024]{1,0:T(8,128)(2,1)S(1)}, bf16[256,1024]{1,0:T(8,128)(2,1)S(1)}, u32[]{:S(2)}, u32[]{:S(2)}) %collective-permute-start.33) | collective-permute-done | bytes 524320 | tf_op jit(solution)/shard_map/ppermute | solution.py:127
  295.8 8.3 %fusion.23 = f32[1024,2048]{1,0:T(8,128)} fusion(bf16[1,1024,2048]{2,1,0:T(8,128)(2,1)S(1)} %constant_dynamic-update-slice_fusion.21, bf16[256,1024]{1,0:T(8,128)(2,1)S(1)} %get-tuple-element.134, bf16[256,1024]{1,0:T(8,128)(2,1)S(1)} %get-tuple-element.133, bf16[512,1024]{1,0:T(8,128)(2,1)S(1)} %add_convert_fusion.3), kind=kOutput, calls=%fused_computation.54 | convolution fusion | flops 4301258752 | bytes 14680064 | tf_op jit(solution)/shard_map/dot_general | solution.py:23
  304.1 9.8 %fusion.33 = bf16[1024,1024]{1,0:T(8,128)(2,1)S(1)} fusion(bf16[1,1024,2048]{1,2,0:T(8,128)(2,1)} %constant_dynamic-update-slice_fusion.28, f32[1024,2048]{1,0:T(8,128)} %fusion.23), kind=kOutput, calls=%fused_computation.96 | convolution fusion | flops 4314890240 | bytes 14680064 | tf_op jit(solution)/shard_map/dot_general | solution.py:31
  313.9 15.5 %fusion.8 = bf16[1024,2048]{1,0:T(8,128)(2,1)} fusion(f32[1024,2048]{1,0:T(8,128)} %fusion.23, bf16[1,1024,2048]{1,2,0:T(8,128)(2,1)} %constant_dynamic-update-slice_fusion.28, bf16[256,1024]{1,0:T(8,128)(2,1)} %get-tuple-element.130, bf16[256,1024]{1,0:T(8,128)(2,1)S(1)} %copy-done.62, bf16[512,1024]{1,0:T(8,128)(2,1)S(1)} %copy-done.19), kind=kOutput, calls=%fused_computation.16 | convolution fusion | flops 4343201792 | bytes 18874368 | tf_op jit(solution)/shard_map/dot_general | solution.py:23
  329.4 12.9 %fusion.176 = (bf16[1,1024,2048]{2,1,0:T(8,128)(2,1)}, f32[1,1024,2048]{2,1,0:T(8,128)}) fusion(f32[1024,2048]{1,0:T(8,128)} %fusion.23, bf16[256,1024]{1,0:T(8,128)(2,1)} %get-tuple-element.130, bf16[256,1024]{1,0:T(8,128)(2,1)S(1)} %copy-done.62, bf16[512,1024]{1,0:T(8,128)(2,1)S(1)} %copy-done.19), kind=kOutput, calls=%fused_computation.434 | convolution fusion | flops 4322230272 | bytes 23068672 | tf_op jit(solution)/shard_map/dot_general | solution.py:27
  342.3 8.1 %fusion.30 = bf16[1024,1024]{1,0:T(8,128)(2,1)S(1)} fusion(bf16[1024,2048]{1,0:T(8,128)(2,1)} %fusion.8, bf16[1,1024,2048]{2,1,0:T(8,128)(2,1)} %copy-done.82), kind=kOutput, calls=%fused_computation.95 | convolution fusion | flops 4296015872 | bytes 10485760 | tf_op jit(solution)/shard_map/dot_general | solution.py:31
  350.4 8.4 %fusion.175 = (bf16[1,1024,2048]{2,1,0:T(8,128)(2,1)}, f32[1,1024,2048]{2,1,0:T(8,128)S(1)}) fusion(bf16[1024,2048]{1,0:T(8,128)(2,1)} %fusion.8, bf16[256,1024]{1,0:T(8,128)(2,1)S(1)} %copy-done.66, bf16[256,1024]{1,0:T(8,128)(2,1)S(1)} %copy-done.64, bf16[512,1024]{1,0:T(8,128)(2,1)S(1)} %add_convert_fusion.3), kind=kOutput, calls=%fused_computation.433 | convolution fusion | flops 4303355904 | bytes 18874368 | tf_op jit(solution)/shard_map/dot_general | solution.py:27
  359.8 2.8 fusion.158
  366.5 4.4 collective-permute-done.109
  373.2 5.2 collective-permute-done.100
  382.4 9.5 %collective-permute-done.110 = bf16[1,128,2048]{2,1,0:T(8,128)(2,1)S(1)} collective-permute-done((bf16[1,128,2048]{2,1,0:T(8,128)(2,1)S(1)}, bf16[1,128,2048]{2,1,0:T(8,128)(2,1)S(1)}, u32[]{:S(2)}, u32[]{:S(2)}) %collective-permute-start.110) | collective-permute-done | bytes 524320 | tf_op jit(solution)/shard_map/ppermute | solution.py:162
  393.9 12.9 %collective-permute-done.101 = bf16[1,128,2048]{2,1,0:T(8,128)(2,1)S(1)} collective-permute-done((bf16[1,128,2048]{2,1,0:T(8,128)(2,1)S(1)}, bf16[1,128,2048]{2,1,0:T(8,128)(2,1)S(1)}, u32[]{:S(2)}, u32[]{:S(2)}) %collective-permute-start.101) | collective-permute-done | bytes 524320 | tf_op jit(solution)/shard_map/ppermute | solution.py:162
  409.0 6.2 collective-permute-done.111
  418.7 5.6 collective-permute-done.59
  433.0 3.0 multiply_add_fusion.2
  443.0 2.5 multiply_convert_fusion.1
  447.8 2.9 convolution_convert_fusion
  454.3 6.0 shard_map.233
  463.7 2.4 collective-permute-done.67
  482.9 2.3 fusion.56
  486.7 8.1 %collective-permute-done.107 = bf16[1,128,2048]{2,1,0:T(8,128)(2,1)S(1)} collective-permute-done((bf16[1,128,2048]{2,1,0:T(8,128)(2,1)S(1)}, bf16[1,128,2048]{2,1,0:T(8,128)(2,1)S(1)}, u32[]{:S(2)}, u32[]{:S(2)}) %collective-permute-start.107) | collective-permute-done | bytes 524320 | tf_op jit(solution)/shard_map/ppermute | solution.py:162
  502.0 2.9 collective-permute-done.94
  510.9 2.7 convolution_convert_fusion.6
  517.0 2.6 copy-done.10
  521.1 8.0 %collective-permute-done.70 = bf16[128,1024]{1,0:T(8,128)(2,1)S(1)} collective-permute-done((bf16[128,1024]{1,0:T(8,128)(2,1)S(1)}, bf16[128,1024]{1,0:T(8,128)(2,1)S(1)}, u32[]{:S(2)}, u32[]{:S(2)}) %collective-permute-start.70) | collective-permute-done | bytes 262176 | tf_op jit(solution)/shard_map/ppermute | solution.py:127
  532.8 2.7 collective-permute-done.62
  535.8 8.6 %fusion.43 = bf16[4,64,1024]{2,1,0:T(8,128)(2,1)S(1)} fusion(bf16[1024,4,64]{0,2,1:T(8,128)(2,1)S(1)} %bitcast.201, f32[4,1024,1024]{1,2,0:T(8,128)} %get-tuple-element.180, f32[4,1024]{1,0:T(4,128)S(1)} %copy-done.69), kind=kOutput, calls=%fused_computation.118 | convolution fusion | flops 545521664 | bytes 17842176 | tf_op jit(solution)/shard_map/hqk,qhd->khd/dot_general | solution.py:81
  544.4 13.4 %multiply_reduce_fusion = (f32[4,1024]{1,0:T(4,128)S(1)}, f32[4,1024,1024]{1,2,0:T(8,128)}) fusion(f32[4,1024,1024]{1,2,0:T(8,128)} %get-tuple-element.180, f32[4,1024]{1,0:T(4,128)S(1)} %copy-done.69, bf16[1024,4,64]{0,2,1:T(8,128)(2,1)S(1)} %bitcast.202, bf16[1024,4,64]{0,2,1:T(8,128)(2,1)S(1)} %bitcast.230), kind=kOutput, calls=%fused_computation.1 | convolution fusion | flops 549449728 | bytes 34635776 | tf_op jit(solution)/shard_map/qhd,khd->hqk/dot_general | solution.py:84
  557.8 7.9 %multiply_convert_fusion = bf16[4,1024,1024]{1,2,0:T(8,128)(2,1)S(1)} fusion(f32[4,1024,1024]{1,2,0:T(8,128)} %get-tuple-element.186, f32[4,1024,1024]{1,2,0:T(8,128)S(1)} %bitcast.200, f32[4,1024]{1,0:T(4,128)S(1)} %get-tuple-element.185, f32[4,1024]{1,0:T(4,128)S(1)} %copy-done.69), kind=kLoop, calls=%fused_computation | loop fusion | flops 16777216 | bytes 41975808 | tf_op jit(solution)/shard_map/convert_element_type | solution.py:88
  565.7 2.7 fusion.48
  577.4 4.1 multiply_reduce_fusion.2
  596.5 2.4 convert_add_fusion.2.in_ref
  598.9 2.9 copy.52
  601.8 6.0 shard_map.236
  616.5 2.4 collective-permute-start.124
  618.9 2.7 collective-permute-start.123
  629.0 3.6 collective-permute-done.77
  644.4 4.0 collective-permute-done.79
  652.4 20.3 %collective-permute-done.65 = bf16[256,1024]{1,0:T(8,128)(2,1)} collective-permute-done((bf16[256,1024]{1,0:T(8,128)(2,1)S(1)}, bf16[256,1024]{1,0:T(8,128)(2,1)}, u32[]{:S(2)}, u32[]{:S(2)}) %collective-permute-start.65) | collective-permute-done | bytes 524320 | tf_op jit(solution)/shard_map/ppermute | solution.py:127
  674.8 4.5 fusion.155
  690.2 3.6 collective-permute-done.83
  698.5 3.2 collective-permute-done.84
  701.8 2.8 collective-permute-start.88
  704.6 3.2 collective-permute-done.88
  707.8 2.5 collective-permute-start.89
  710.4 3.2 collective-permute-done.89
  714.5 3.4 multiply_add_fusion.in_ref
  717.8 6.5 shard_map.235
  (664 shorter events, 289.4 us)
Async XLA Ops:
  2.5 68.4 %collective-permute-start.6 = (bf16[3,128,256]{2,1,0:T(8,128)(2,1)}, bf16[3,128,256]{2,1,0:T(8,128)(2,1)}, u32[]{:S(2)}, u32[]{:S(2)}) collective-permute-start(bf16[3,128,256]{2,1,0:T(8,128)(2,1)} %get-tuple-element.66), channel_id=1, source_target_pairs={{0,8},{8,16},{16,24},{24,28},{28,20},{20,12},{12,4},{4,0},{1,9},{9... | collective-permute-start | bytes 589832 | tf_op jit(solution)/shard_map/ppermute | solution.py:162
  5.5 65.7 %collective-permute-start.2 = (bf16[3,128,256]{2,1,0:T(8,128)(2,1)}, bf16[3,128,256]{2,1,0:T(8,128)(2,1)}, u32[]{:S(2)}, u32[]{:S(2)}) collective-permute-start(bf16[3,128,256]{2,1,0:T(8,128)(2,1)} %get-tuple-element.66), channel_id=1, source_target_pairs={{0,4},{8,0},{16,8},{24,16},{28,24},{20,28},{12,20},{4,12},{1,5},{9... | collective-permute-start | bytes 589832 | tf_op jit(solution)/shard_map/ppermute | solution.py:162
  13.8 59.2 %collective-permute-start.21 = (bf16[128,1024]{1,0:T(8,128)(2,1)}, bf16[128,1024]{1,0:T(8,128)(2,1)}, u32[]{:S(2)}, u32[]{:S(2)}) collective-permute-start(bf16[128,1024]{1,0:T(8,128)(2,1)} %constant_dynamic-slice_fusion.9), channel_id=1, source_target_pairs={{0,2},{2,0},{1,3},{3,1},{4,6},{6,4},{5,7},{7,5},{8,10},{10,8},{9,1... | collective-permute-start | bytes 786440 | tf_op jit(solution)/shard_map/ppermute | solution.py:127
  23.6 57.1 %collective-permute-start = (bf16[256,1024]{1,0:T(8,128)(2,1)}, bf16[256,1024]{1,0:T(8,128)(2,1)}, u32[]{:S(2)}, u32[]{:S(2)}) collective-permute-start(bf16[256,1024]{1,0:T(8,128)(2,1)} %constant_dynamic-slice_fusion.14), channel_id=1, source_target_pairs={{0,2},{2,0},{1,3},{3,1},{4,6},{6,4},{5,7},{7,5},{8,10},{10,8},{9,1... | collective-permute-start | bytes 1572872 | tf_op jit(solution)/shard_map/ppermute | solution.py:127
  31.5 66.1 %collective-permute-start.55 = (bf16[256,1024]{1,0:T(8,128)(2,1)}, bf16[256,1024]{1,0:T(8,128)(2,1)}, u32[]{:S(2)}, u32[]{:S(2)}) collective-permute-start(bf16[256,1024]{1,0:T(8,128)(2,1)} %constant_dynamic-slice_fusion.4), channel_id=1, source_target_pairs={{0,2},{2,0},{1,3},{3,1},{4,6},{6,4},{5,7},{7,5},{8,10},{10,8},{9,1... | collective-permute-start | bytes 1572872 | tf_op jit(solution)/shard_map/ppermute | solution.py:127
  80.7 28.9 %collective-permute-start.1 = (bf16[256,1024]{1,0:T(8,128)(2,1)}, bf16[256,1024]{1,0:T(8,128)(2,1)S(1)}, u32[]{:S(2)}, u32[]{:S(2)}) collective-permute-start(bf16[256,1024]{1,0:T(8,128)(2,1)} %collective-permute-done), channel_id=1, source_target_pairs={{0,1},{1,0},{2,3},{3,2},{4,5},{5,4},{6,7},{7,6},{8,9},{9,8},{10,11... | collective-permute-start | bytes 1572872 | tf_op jit(solution)/shard_map/ppermute | solution.py:127
  101.7 66.6 %collective-permute-start.56 = (bf16[256,1024]{1,0:T(8,128)(2,1)}, bf16[256,1024]{1,0:T(8,128)(2,1)}, u32[]{:S(2)}, u32[]{:S(2)}) collective-permute-start(bf16[256,1024]{1,0:T(8,128)(2,1)} %collective-permute-done.55), channel_id=1, source_target_pairs={{0,1},{1,0},{2,3},{3,2},{4,5},{5,4},{6,7},{7,6},{8,9},{9,8},{10,11... | collective-permute-start | bytes 1572872 | tf_op jit(solution)/shard_map/ppermute | solution.py:127
  106.1 43.9 %collective-permute-start.12 = (bf16[3,128,256]{1,2,0:T(8,128)(2,1)}, bf16[3,128,256]{1,2,0:T(8,128)(2,1)}, u32[]{:S(2)}, u32[]{:S(2)}) collective-permute-start(bf16[3,128,256]{1,2,0:T(8,128)(2,1)} %collective-permute-done.11), channel_id=1, source_target_pairs={{0,4},{8,0},{16,8},{24,16},{28,24},{20,28},{12,20},{4,12},{1,5},{9... | collective-permute-start | bytes 589832 | tf_op jit(solution)/shard_map/ppermute | solution.py:162
  106.4 42.4 %collective-permute-start.16 = (bf16[3,128,256]{1,2,0:T(8,128)(2,1)}, bf16[3,128,256]{1,2,0:T(8,128)(2,1)}, u32[]{:S(2)}, u32[]{:S(2)}) collective-permute-start(bf16[3,128,256]{1,2,0:T(8,128)(2,1)} %collective-permute-done.15), channel_id=1, source_target_pairs={{0,8},{8,16},{16,24},{24,28},{28,20},{20,12},{12,4},{4,0},{1,9},{9... | collective-permute-start | bytes 589832 | tf_op jit(solution)/shard_map/ppermute | solution.py:162
  109.1 37.0 %collective-permute-start.25 = (bf16[2,128,256]{1,2,0:T(8,128)(2,1)}, bf16[2,128,256]{1,2,0:T(8,128)(2,1)}, u32[]{:S(2)}, u32[]{:S(2)}) collective-permute-start(bf16[2,128,256]{1,2,0:T(8,128)(2,1)} %collective-permute-done.24), channel_id=1, source_target_pairs={{0,4},{8,0},{16,8},{24,16},{28,24},{20,28},{12,20},{4,12},{1,5},{9... | collective-permute-start | bytes 393224 | tf_op jit(solution)/shard_map/ppermute | solution.py:162
  110.1 34.8 %collective-permute-start.29 = (bf16[2,128,256]{1,2,0:T(8,128)(2,1)}, bf16[2,128,256]{1,2,0:T(8,128)(2,1)S(1)}, u32[]{:S(2)}, u32[]{:S(2)}) collective-permute-start(bf16[2,128,256]{1,2,0:T(8,128)(2,1)} %collective-permute-done.28), channel_id=1, source_target_pairs={{0,8},{8,16},{16,24},{24,28},{28,20},{20,12},{12,4},{4,0},{1,9},{9... | collective-permute-start | bytes 393224 | tf_op jit(solution)/shard_map/ppermute | solution.py:162
  163.9 45.9 %collective-permute-start.19 = (bf16[3,1024,256]{1,2,0:T(8,128)(2,1)S(1)}, bf16[3,1024,256]{1,2,0:T(8,128)(2,1)S(1)}, u32[]{:S(2)}, u32[]{:S(2)}) collective-permute-start(bf16[3,1024,256]{1,2,0:T(8,128)(2,1)S(1)} %constant_dynamic-update-slice_fusion.7), channel_id=1, source_target_pairs={{0,2},{2,0},{1,3},{3,1},{4,6},{6,4},{5,7},{7,5},{8,10},{10,8},{9,1... | collective-permute-start | bytes 4718600 | tf_op jit(solution)/shard_map/ppermute | solution.py:127
  165.1 44.6 %collective-permute-start.31 = (bf16[512,512]{0,1:T(8,128)(2,1)S(1)}, bf16[512,512]{0,1:T(8,128)(2,1)S(1)}, u32[]{:S(2)}, u32[]{:S(2)}) collective-permute-start(bf16[512,512]{0,1:T(8,128)(2,1)S(1)} %fusion.79), channel_id=1, source_target_pairs={{0,2},{2,0},{1,3},{3,1},{4,6},{6,4},{5,7},{7,5},{8,10},{10,8},{9,1... | collective-permute-start | bytes 1572872 | tf_op jit(solution)/shard_map/ppermute | solution.py:127
  167.1 47.3 %collective-permute-start.10 = (bf16[512,256]{0,1:T(8,128)(2,1)S(1)}, bf16[512,256]{0,1:T(8,128)(2,1)S(1)}, u32[]{:S(2)}, u32[]{:S(2)}) collective-permute-start(bf16[512,256]{0,1:T(8,128)(2,1)S(1)} %bitcast.235), channel_id=1, source_target_pairs={{0,2},{2,0},{1,3},{3,1},{4,6},{6,4},{5,7},{7,5},{8,10},{10,8},{9,1... | collective-permute-start | bytes 786440 | tf_op jit(solution)/shard_map/ppermute | solution.py:127
  210.3 14.1 %collective-permute-start.39 = (bf16[1,128,2048]{2,1,0:T(8,128)(2,1)S(1)}, bf16[1,128,2048]{2,1,0:T(8,128)(2,1)S(1)}, u32[]{:S(2)}, u32[]{:S(2)}) collective-permute-start(bf16[1,128,2048]{2,1,0:T(8,128)(2,1)S(1)} %dynamic-slice_bitcast_fusion.1), channel_id=1, source_target_pairs={{0,8},{8,16},{16,24},{24,28},{28,20},{20,12},{12,4},{4,0},{1,9},{9... | collective-permute-start | bytes 1572872 | tf_op jit(solution)/shard_map/ppermute | solution.py:162
  211.4 13.5 %collective-permute-start.35 = (bf16[1,128,2048]{2,1,0:T(8,128)(2,1)S(1)}, bf16[1,128,2048]{2,1,0:T(8,128)(2,1)S(1)}, u32[]{:S(2)}, u32[]{:S(2)}) collective-permute-start(bf16[1,128,2048]{2,1,0:T(8,128)(2,1)S(1)} %dynamic-slice_bitcast_fusion.1), channel_id=1, source_target_pairs={{0,4},{8,0},{16,8},{24,16},{28,24},{20,28},{12,20},{4,12},{1,5},{9... | collective-permute-start | bytes 1572872 | tf_op jit(solution)/shard_map/ppermute | solution.py:162
  212.4 23.3 %collective-permute-start.47 = (bf16[1,128,2048]{1,2,0:T(8,128)(2,1)S(1)}, bf16[1,128,2048]{1,2,0:T(8,128)(2,1)S(1)}, u32[]{:S(2)}, u32[]{:S(2)}) collective-permute-start(bf16[1,128,2048]{1,2,0:T(8,128)(2,1)S(1)} %dynamic-slice_bitcast_fusion), channel_id=1, source_target_pairs={{0,8},{8,16},{16,24},{24,28},{28,20},{20,12},{12,4},{4,0},{1,9},{9... | collective-permute-start | bytes 1572872 | tf_op jit(solution)/shard_map/ppermute | solution.py:162
  213.5 22.7 %collective-permute-start.43 = (bf16[1,128,2048]{1,2,0:T(8,128)(2,1)S(1)}, bf16[1,128,2048]{1,2,0:T(8,128)(2,1)S(1)}, u32[]{:S(2)}, u32[]{:S(2)}) collective-permute-start(bf16[1,128,2048]{1,2,0:T(8,128)(2,1)S(1)} %dynamic-slice_bitcast_fusion), channel_id=1, source_target_pairs={{0,4},{8,0},{16,8},{24,16},{28,24},{20,28},{12,20},{4,12},{1,5},{9... | collective-permute-start | bytes 1572872 | tf_op jit(solution)/shard_map/ppermute | solution.py:162
  215.2 45.2 %collective-permute-start.20 = (bf16[512,1024]{1,0:T(8,128)(2,1)S(1)}, bf16[512,1024]{1,0:T(8,128)(2,1)S(1)}, u32[]{:S(2)}, u32[]{:S(2)}) collective-permute-start(bf16[512,1024]{1,0:T(8,128)(2,1)S(1)} %convolution_convert_fusion.2), channel_id=1, source_target_pairs={{0,1},{1,0},{2,3},{3,2},{4,5},{5,4},{6,7},{7,6},{8,9},{9,8},{10,11... | collective-permute-start | bytes 3145736 | tf_op jit(solution)/shard_map/ppermute | solution.py:127
  224.4 22.5 %collective-permute-start.40 = (bf16[1,128,2048]{2,1,0:T(8,128)(2,1)S(1)}, bf16[1,128,2048]{2,1,0:T(8,128)(2,1)S(1)}, u32[]{:S(2)}, u32[]{:S(2)}) collective-permute-start(bf16[1,128,2048]{2,1,0:T(8,128)(2,1)S(1)} %collective-permute-done.39), channel_id=1, source_target_pairs={{0,8},{8,16},{16,24},{24,28},{28,20},{20,12},{12,4},{4,0},{1,9},{9... | collective-permute-start | bytes 1572872 | tf_op jit(solution)/shard_map/ppermute | solution.py:162
  224.9 22.5 %collective-permute-start.36 = (bf16[1,128,2048]{2,1,0:T(8,128)(2,1)S(1)}, bf16[1,128,2048]{2,1,0:T(8,128)(2,1)S(1)}, u32[]{:S(2)}, u32[]{:S(2)}) collective-permute-start(bf16[1,128,2048]{2,1,0:T(8,128)(2,1)S(1)} %collective-permute-done.35), channel_id=1, source_target_pairs={{0,4},{8,0},{16,8},{24,16},{28,24},{20,28},{12,20},{4,12},{1,5},{9... | collective-permute-start | bytes 1572872 | tf_op jit(solution)/shard_map/ppermute | solution.py:162
  235.6 22.5 %collective-permute-start.48 = (bf16[1,128,2048]{1,2,0:T(8,128)(2,1)S(1)}, bf16[1,128,2048]{1,2,0:T(8,128)(2,1)S(1)}, u32[]{:S(2)}, u32[]{:S(2)}) collective-permute-start(bf16[1,128,2048]{1,2,0:T(8,128)(2,1)S(1)} %collective-permute-done.47), channel_id=1, source_target_pairs={{0,8},{8,16},{16,24},{24,28},{28,20},{20,12},{12,4},{4,0},{1,9},{9... | collective-permute-start | bytes 1572872 | tf_op jit(solution)/shard_map/ppermute | solution.py:162
  236.2 22.5 %collective-permute-start.44 = (bf16[1,128,2048]{1,2,0:T(8,128)(2,1)S(1)}, bf16[1,128,2048]{1,2,0:T(8,128)(2,1)S(1)}, u32[]{:S(2)}, u32[]{:S(2)}) collective-permute-start(bf16[1,128,2048]{1,2,0:T(8,128)(2,1)S(1)} %collective-permute-done.43), channel_id=1, source_target_pairs={{0,4},{8,0},{16,8},{24,16},{28,24},{20,28},{12,20},{4,12},{1,5},{9... | collective-permute-start | bytes 1572872 | tf_op jit(solution)/shard_map/ppermute | solution.py:162
  246.9 20.6 %collective-permute-start.41 = (bf16[1,128,2048]{2,1,0:T(8,128)(2,1)S(1)}, bf16[1,128,2048]{2,1,0:T(8,128)(2,1)S(1)}, u32[]{:S(2)}, u32[]{:S(2)}) collective-permute-start(bf16[1,128,2048]{2,1,0:T(8,128)(2,1)S(1)} %collective-permute-done.40), channel_id=1, source_target_pairs={{0,8},{8,16},{16,24},{24,28},{28,20},{20,12},{12,4},{4,0},{1,9},{9... | collective-permute-start | bytes 1572872 | tf_op jit(solution)/shard_map/ppermute | solution.py:162
  247.4 20.7 %collective-permute-start.37 = (bf16[1,128,2048]{2,1,0:T(8,128)(2,1)S(1)}, bf16[1,128,2048]{2,1,0:T(8,128)(2,1)S(1)}, u32[]{:S(2)}, u32[]{:S(2)}) collective-permute-start(bf16[1,128,2048]{2,1,0:T(8,128)(2,1)S(1)} %collective-permute-done.36), channel_id=1, source_target_pairs={{0,4},{8,0},{16,8},{24,16},{28,24},{20,28},{12,20},{4,12},{1,5},{9... | collective-permute-start | bytes 1572872 | tf_op jit(solution)/shard_map/ppermute | solution.py:162
  258.1 15.3 %collective-permute-start.49 = (bf16[1,128,2048]{1,2,0:T(8,128)(2,1)S(1)}, bf16[1,128,2048]{1,2,0:T(8,128)(2,1)S(1)}, u32[]{:S(2)}, u32[]{:S(2)}) collective-permute-start(bf16[1,128,2048]{1,2,0:T(8,128)(2,1)S(1)} %collective-permute-done.48), channel_id=1, source_target_pairs={{0,8},{8,16},{16,24},{24,28},{28,20},{20,12},{12,4},{4,0},{1,9},{9... | collective-permute-start | bytes 1572872 | tf_op jit(solution)/shard_map/ppermute | solution.py:162
  258.6 15.9 %collective-permute-start.45 = (bf16[1,128,2048]{1,2,0:T(8,128)(2,1)S(1)}, bf16[1,128,2048]{1,2,0:T(8,128)(2,1)S(1)}, u32[]{:S(2)}, u32[]{:S(2)}) collective-permute-start(bf16[1,128,2048]{1,2,0:T(8,128)(2,1)S(1)} %collective-permute-done.44), channel_id=1, source_target_pairs={{0,4},{8,0},{16,8},{24,16},{28,24},{20,28},{12,20},{4,12},{1,5},{9... | collective-permute-start | bytes 1572872 | tf_op jit(solution)/shard_map/ppermute | solution.py:162
  267.4 12.5 %collective-permute-start.32 = (bf16[512,1024]{1,0:T(8,128)(2,1)S(1)}, bf16[512,1024]{1,0:T(8,128)(2,1)S(1)}, u32[]{:S(2)}, u32[]{:S(2)}) collective-permute-start(bf16[512,1024]{1,0:T(8,128)(2,1)S(1)} %convolution_convert_fusion.1), channel_id=1, source_target_pairs={{0,1},{1,0},{2,3},{3,2},{4,5},{5,4},{6,7},{7,6},{8,9},{9,8},{10,11... | collective-permute-start | bytes 3145736 | tf_op jit(solution)/shard_map/ppermute | solution.py:127
  359.0 22.4 %collective-permute-start.52 = (bf16[256,1024]{1,0:T(8,128)(2,1)S(1)}, bf16[256,1024]{1,0:T(8,128)(2,1)S(1)}, u32[]{:S(2)}, u32[]{:S(2)}) collective-permute-start(bf16[256,1024]{1,0:T(8,128)(2,1)S(1)} %constant_dynamic-slice_fusion.5), channel_id=1, source_target_pairs={{0,1},{1,0},{2,3},{3,2},{4,5},{5,4},{6,7},{7,6},{8,9},{9,8},{10,11... | collective-permute-start | bytes 1572872 | tf_op jit(solution)/shard_map/ppermute | solution.py:127
  364.7 28.7 %collective-permute-start.58 = (bf16[256,1024]{1,0:T(8,128)(2,1)S(1)}, bf16[256,1024]{1,0:T(8,128)(2,1)S(1)}, u32[]{:S(2)}, u32[]{:S(2)}) collective-permute-start(bf16[256,1024]{1,0:T(8,128)(2,1)S(1)} %constant_dynamic-slice_fusion.3), channel_id=1, source_target_pairs={{0,1},{1,0},{2,3},{3,2},{4,5},{5,4},{6,7},{7,6},{8,9},{9,8},{10,11... | collective-permute-start | bytes 1572872 | tf_op jit(solution)/shard_map/ppermute | solution.py:127
  364.8 64.0 %collective-permute-start.57 = (bf16[512,1024]{1,0:T(8,128)(2,1)S(1)}, bf16[512,1024]{1,0:T(8,128)(2,1)S(1)}, u32[]{:S(2)}, u32[]{:S(2)}) collective-permute-start(bf16[512,1024]{1,0:T(8,128)(2,1)S(1)} %get-tuple-element.103), channel_id=1, source_target_pairs={{0,1},{1,0},{2,3},{3,2},{4,5},{5,4},{6,7},{7,6},{8,9},{9,8},{10,11... | collective-permute-start | bytes 3145736 | tf_op jit(solution)/shard_map/ppermute | solution.py:127
  378.4 29.1 %collective-permute-start.114 = (bf16[1,128,2048]{2,1,0:T(8,128)(2,1)S(1)}, bf16[1,128,2048]{2,1,0:T(8,128)(2,1)S(1)}, u32[]{:S(2)}, u32[]{:S(2)}) collective-permute-start(bf16[1,128,2048]{2,1,0:T(8,128)(2,1)S(1)} %pad_maximum_fusion.22), channel_id=1, source_target_pairs={{0,4},{8,0},{16,8},{24,16},{28,24},{20,28},{12,20},{4,12},{1,5},{9... | collective-permute-start | bytes 1572872 | tf_op jit(solution)/shard_map/ppermute | solution.py:162
  381.4 36.5 %collective-permute-start.105 = (bf16[1,128,2048]{2,1,0:T(8,128)(2,1)S(1)}, bf16[1,128,2048]{2,1,0:T(8,128)(2,1)S(1)}, u32[]{:S(2)}, u32[]{:S(2)}) collective-permute-start(bf16[1,128,2048]{2,1,0:T(8,128)(2,1)S(1)} %pad_maximum_fusion.20), channel_id=1, source_target_pairs={{0,4},{8,0},{16,8},{24,16},{28,24},{20,28},{12,20},{4,12},{1,5},{9... | collective-permute-start | bytes 1572872 | tf_op jit(solution)/shard_map/ppermute | solution.py:162
  392.0 14.9 %collective-permute-start.101 = (bf16[1,128,2048]{2,1,0:T(8,128)(2,1)S(1)}, bf16[1,128,2048]{2,1,0:T(8,128)(2,1)S(1)}, u32[]{:S(2)}, u32[]{:S(2)}) collective-permute-start(bf16[1,128,2048]{2,1,0:T(8,128)(2,1)S(1)} %pad_maximum_fusion.19), channel_id=1, source_target_pairs={{0,8},{8,16},{16,24},{24,28},{28,20},{20,12},{12,4},{4,0},{1,9},{9... | collective-permute-start | bytes 1572872 | tf_op jit(solution)/shard_map/ppermute | solution.py:162
  393.4 21.9 %collective-permute-start.111 = (bf16[1,128,2048]{2,1,0:T(8,128)(2,1)S(1)}, bf16[1,128,2048]{2,1,0:T(8,128)(2,1)S(1)}, u32[]{:S(2)}, u32[]{:S(2)}) collective-permute-start(bf16[1,128,2048]{2,1,0:T(8,128)(2,1)S(1)} %fusion.54), channel_id=1, source_target_pairs={{0,8},{8,16},{16,24},{24,28},{28,20},{20,12},{12,4},{4,0},{1,9},{9... | collective-permute-start | bytes 1572872 | tf_op jit(solution)/shard_map/ppermute | solution.py:162
  407.5 16.8 %collective-permute-start.59 = (bf16[256,1024]{1,0:T(8,128)(2,1)S(1)}, bf16[256,1024]{1,0:T(8,128)(2,1)S(1)}, u32[]{:S(2)}, u32[]{:S(2)}) collective-permute-start(bf16[256,1024]{1,0:T(8,128)(2,1)S(1)} %add_convert_fusion.6), channel_id=1, source_target_pairs={{0,2},{2,0},{1,3},{3,1},{4,6},{6,4},{5,7},{7,5},{8,10},{10,8},{9,1... | collective-permute-start | bytes 1572872 | tf_op jit(solution)/shard_map/ppermute | solution.py:127
  417.9 15.1 %collective-permute-start.51 = (bf16[512,1024]{1,0:T(8,128)(2,1)S(1)}, bf16[512,1024]{1,0:T(8,128)(2,1)S(1)}, u32[]{:S(2)}, u32[]{:S(2)}) collective-permute-start(bf16[512,1024]{1,0:T(8,128)(2,1)S(1)} %get-tuple-element.106), channel_id=1, source_target_pairs={{0,1},{1,0},{2,3},{3,2},{4,5},{5,4},{6,7},{7,6},{8,9},{9,8},{10,11... | collective-permute-start | bytes 3145736 | tf_op jit(solution)/shard_map/ppermute | solution.py:127
  418.7 12.8 %collective-permute-start.54 = (bf16[256,1024]{1,0:T(8,128)(2,1)S(1)}, bf16[256,1024]{1,0:T(8,128)(2,1)S(1)}, u32[]{:S(2)}, u32[]{:S(2)}) collective-permute-start(bf16[256,1024]{1,0:T(8,128)(2,1)S(1)} %collective-permute-done.53), channel_id=1, source_target_pairs={{0,1},{1,0},{2,3},{3,2},{4,5},{5,4},{6,7},{7,6},{8,9},{9,8},{10,11... | collective-permute-start | bytes 1572872 | tf_op jit(solution)/shard_map/ppermute | solution.py:127
  425.5 56.9 %collective-permute-start.112 = (bf16[1,128,2048]{2,1,0:T(8,128)(2,1)}, bf16[1,128,2048]{2,1,0:T(8,128)(2,1)}, u32[]{:S(2)}, u32[]{:S(2)}) collective-permute-start(bf16[1,128,2048]{2,1,0:T(8,128)(2,1)} %get-tuple-element.67), channel_id=1, source_target_pairs={{0,8},{8,16},{16,24},{24,28},{28,20},{20,12},{12,4},{4,0},{1,9},{9... | collective-permute-start | bytes 1572872 | tf_op jit(solution)/shard_map/ppermute | solution.py:162
  427.6 32.8 %collective-permute-start.115 = (bf16[1,128,2048]{2,1,0:T(8,128)(2,1)}, bf16[1,128,2048]{2,1,0:T(8,128)(2,1)}, u32[]{:S(2)}, u32[]{:S(2)}) collective-permute-start(bf16[1,128,2048]{2,1,0:T(8,128)(2,1)} %get-tuple-element.68), channel_id=1, source_target_pairs={{0,4},{8,0},{16,8},{24,16},{28,24},{20,28},{12,20},{4,12},{1,5},{9... | collective-permute-start | bytes 1572872 | tf_op jit(solution)/shard_map/ppermute | solution.py:162
  428.8 56.4 %collective-permute-start.103 = (bf16[1,128,2048]{2,1,0:T(8,128)(2,1)}, bf16[1,128,2048]{2,1,0:T(8,128)(2,1)}, u32[]{:S(2)}, u32[]{:S(2)}) collective-permute-start(bf16[1,128,2048]{2,1,0:T(8,128)(2,1)} %get-tuple-element.71), channel_id=1, source_target_pairs={{0,8},{8,16},{16,24},{24,28},{28,20},{20,12},{12,4},{4,0},{1,9},{9... | collective-permute-start | bytes 1572872 | tf_op jit(solution)/shard_map/ppermute | solution.py:162
  431.5 30.8 %collective-permute-start.106 = (bf16[1,128,2048]{2,1,0:T(8,128)(2,1)}, bf16[1,128,2048]{2,1,0:T(8,128)(2,1)}, u32[]{:S(2)}, u32[]{:S(2)}) collective-permute-start(bf16[1,128,2048]{2,1,0:T(8,128)(2,1)} %get-tuple-element.72), channel_id=1, source_target_pairs={{0,4},{8,0},{16,8},{24,16},{28,24},{20,28},{12,20},{4,12},{1,5},{9... | collective-permute-start | bytes 1572872 | tf_op jit(solution)/shard_map/ppermute | solution.py:162
  453.8 12.4 %collective-permute-start.67 = (bf16[512,512]{0,1:T(8,128)(2,1)}, bf16[512,512]{0,1:T(8,128)(2,1)}, u32[]{:S(2)}, u32[]{:S(2)}) collective-permute-start(bf16[512,512]{0,1:T(8,128)(2,1)} %fusion.78), channel_id=1, source_target_pairs={{0,2},{2,0},{1,3},{3,1},{4,6},{6,4},{5,7},{7,5},{8,10},{10,8},{9,1... | collective-permute-start | bytes 1572872 | tf_op jit(solution)/shard_map/ppermute | solution.py:127
  461.9 20.5 %collective-permute-start.116 = (bf16[1,128,2048]{2,1,0:T(8,128)(2,1)S(1)}, bf16[1,128,2048]{2,1,0:T(8,128)(2,1)S(1)}, u32[]{:S(2)}, u32[]{:S(2)}) collective-permute-start(bf16[1,128,2048]{2,1,0:T(8,128)(2,1)S(1)} %fusion.53), channel_id=1, source_target_pairs={{0,4},{8,0},{16,8},{24,16},{28,24},{20,28},{12,20},{4,12},{1,5},{9... | collective-permute-start | bytes 1572872 | tf_op jit(solution)/shard_map/ppermute | solution.py:162
  480.4 26.8 %collective-permute-start.61 = (bf16[512,1024]{1,0:T(8,128)(2,1)S(1)}, bf16[512,1024]{1,0:T(8,128)(2,1)S(1)}, u32[]{:S(2)}, u32[]{:S(2)}) collective-permute-start(bf16[512,1024]{1,0:T(8,128)(2,1)S(1)} %copy-done.30), channel_id=1, source_target_pairs={{0,1},{1,0},{2,3},{3,2},{4,5},{5,4},{6,7},{7,6},{8,9},{9,8},{10,11... | collective-permute-start | bytes 3145736 | tf_op jit(solution)/shard_map/ppermute | solution.py:127
  481.3 13.5 %collective-permute-start.107 = (bf16[1,128,2048]{2,1,0:T(8,128)(2,1)S(1)}, bf16[1,128,2048]{2,1,0:T(8,128)(2,1)S(1)}, u32[]{:S(2)}, u32[]{:S(2)}) collective-permute-start(bf16[1,128,2048]{2,1,0:T(8,128)(2,1)S(1)} %fusion.58), channel_id=1, source_target_pairs={{0,4},{8,0},{16,8},{24,16},{28,24},{20,28},{12,20},{4,12},{1,5},{9... | collective-permute-start | bytes 1572872 | tf_op jit(solution)/shard_map/ppermute | solution.py:162
  482.3 18.4 %collective-permute-start.69 = (bf16[128,1024]{1,0:T(8,128)(2,1)S(1)}, bf16[128,1024]{1,0:T(8,128)(2,1)S(1)}, u32[]{:S(2)}, u32[]{:S(2)}) collective-permute-start(bf16[128,1024]{1,0:T(8,128)(2,1)S(1)} %constant_dynamic-slice_fusion.1), channel_id=1, source_target_pairs={{0,1},{1,0},{2,3},{3,2},{4,5},{5,4},{6,7},{7,6},{8,9},{9,8},{10,11... | collective-permute-start | bytes 786440 | tf_op jit(solution)/shard_map/ppermute | solution.py:127
  482.4 114.0 %collective-permute-start.68 = (bf16[256,1024]{1,0:T(8,128)(2,1)}, bf16[256,1024]{1,0:T(8,128)(2,1)}, u32[]{:S(2)}, u32[]{:S(2)}) collective-permute-start(bf16[256,1024]{1,0:T(8,128)(2,1)} %get-tuple-element.124), channel_id=1, source_target_pairs={{0,1},{1,0},{2,3},{3,2},{4,5},{5,4},{6,7},{7,6},{8,9},{9,8},{10,11... | collective-permute-start | bytes 1572872 | tf_op jit(solution)/shard_map/ppermute | solution.py:127
  485.3 12.6 %collective-permute-start.93 = (bf16[2,128,256]{1,2,0:T(8,128)(2,1)S(1)}, bf16[2,128,256]{1,2,0:T(8,128)(2,1)S(1)}, u32[]{:S(2)}, u32[]{:S(2)}) collective-permute-start(bf16[2,128,256]{1,2,0:T(8,128)(2,1)S(1)} %get-tuple-element.95), channel_id=1, source_target_pairs={{0,8},{8,16},{16,24},{24,28},{28,20},{20,12},{12,4},{4,0},{1,9},{9... | collective-permute-start | bytes 393224 | tf_op jit(solution)/shard_map/ppermute | solution.py:162
  497.9 87.7 %collective-permute-start.117 = (bf16[1,128,2048]{2,1,0:T(8,128)(2,1)}, bf16[1,128,2048]{2,1,0:T(8,128)(2,1)}, u32[]{:S(2)}, u32[]{:S(2)}) collective-permute-start(bf16[1,128,2048]{2,1,0:T(8,128)(2,1)} %fusion.56), channel_id=1, source_target_pairs={{0,2},{2,0},{1,3},{3,1},{4,6},{6,4},{5,7},{7,5},{8,10},{10,8},{9,1... | collective-permute-start | bytes 1572872 | tf_op jit(solution)/shard_map/ppermute | solution.py:127
  504.8 84.2 %collective-permute-start.108 = (bf16[1,128,2048]{2,1,0:T(8,128)(2,1)}, bf16[1,128,2048]{2,1,0:T(8,128)(2,1)}, u32[]{:S(2)}, u32[]{:S(2)}) collective-permute-start(bf16[1,128,2048]{2,1,0:T(8,128)(2,1)} %fusion.61), channel_id=1, source_target_pairs={{0,2},{2,0},{1,3},{3,1},{4,6},{6,4},{5,7},{7,5},{8,10},{10,8},{9,1... | collective-permute-start | bytes 1572872 | tf_op jit(solution)/shard_map/ppermute | solution.py:127
  506.3 22.8 %collective-permute-start.70 = (bf16[128,1024]{1,0:T(8,128)(2,1)S(1)}, bf16[128,1024]{1,0:T(8,128)(2,1)S(1)}, u32[]{:S(2)}, u32[]{:S(2)}) collective-permute-start(bf16[128,1024]{1,0:T(8,128)(2,1)S(1)} %add_convert_fusion.8), channel_id=1, source_target_pairs={{0,2},{2,0},{1,3},{3,1},{4,6},{6,4},{5,7},{7,5},{8,10},{10,8},{9,1... | collective-permute-start | bytes 786440 | tf_op jit(solution)/shard_map/ppermute | solution.py:127
  507.2 24.7 %collective-permute-start.99 = (bf16[2,128,256]{1,2,0:T(8,128)(2,1)S(1)}, bf16[2,128,256]{1,2,0:T(8,128)(2,1)S(1)}, u32[]{:S(2)}, u32[]{:S(2)}) collective-permute-start(bf16[2,128,256]{1,2,0:T(8,128)(2,1)S(1)} %fusion.113), channel_id=1, source_target_pairs={{0,2},{2,0},{1,3},{3,1},{4,6},{6,4},{5,7},{7,5},{8,10},{10,8},{9,1... | collective-permute-start | bytes 393224 | tf_op jit(solution)/shard_map/ppermute | solution.py:127
  531.9 60.0 %collective-permute-start.71 = (bf16[128,1024]{1,0:T(8,128)(2,1)S(1)}, bf16[128,1024]{1,0:T(8,128)(2,1)}, u32[]{:S(2)}, u32[]{:S(2)}) collective-permute-start(bf16[128,1024]{1,0:T(8,128)(2,1)S(1)} %collective-permute-done.70), channel_id=1, source_target_pairs={{0,1},{1,0},{2,3},{3,2},{4,5},{5,4},{6,7},{7,6},{8,9},{9,8},{10,11... | collective-permute-start | bytes 786440 | tf_op jit(solution)/shard_map/ppermute | solution.py:127
  575.6 32.9 %collective-permute-start.72 = (bf16[3,128,128]{1,2,0:T(8,128)(2,1)}, bf16[3,128,128]{1,2,0:T(8,128)(2,1)}, u32[]{:S(2)}, u32[]{:S(2)}) collective-permute-start(bf16[3,128,128]{1,2,0:T(8,128)(2,1)} %get-tuple-element.111), channel_id=1, source_target_pairs={{0,8},{8,16},{16,24},{24,28},{28,20},{20,12},{12,4},{4,0},{1,9},{9... | collective-permute-start | bytes 294920 | tf_op jit(solution)/shard_map/ppermute | solution.py:162
  585.5 23.0 %collective-permute-start.76 = (bf16[3,128,128]{1,2,0:T(8,128)(2,1)}, bf16[3,128,128]{1,2,0:T(8,128)(2,1)}, u32[]{:S(2)}, u32[]{:S(2)}) collective-permute-start(bf16[3,128,128]{1,2,0:T(8,128)(2,1)} %get-tuple-element.112), channel_id=1, source_target_pairs={{0,4},{8,0},{16,8},{24,16},{28,24},{20,28},{12,20},{4,12},{1,5},{9... | collective-permute-start | bytes 294920 | tf_op jit(solution)/shard_map/ppermute | solution.py:162
  591.9 45.7 %collective-permute-start.64 = (bf16[256,1024]{1,0:T(8,128)(2,1)}, bf16[256,1024]{1,0:T(8,128)(2,1)}, u32[]{:S(2)}, u32[]{:S(2)}) collective-permute-start(bf16[256,1024]{1,0:T(8,128)(2,1)} %constant_dynamic-slice_fusion.2), channel_id=1, source_target_pairs={{0,1},{1,0},{2,3},{3,2},{4,5},{5,4},{6,7},{7,6},{8,9},{9,8},{10,11... | collective-permute-start | bytes 1572872 | tf_op jit(solution)/shard_map/ppermute | solution.py:127
  594.8 12.9 %collective-permute-start.119 = (f32[8,1024]{1,0:T(8,128)S(1)}, f32[8,1024]{1,0:T(8,128)}, u32[]{:S(2)}, u32[]{:S(2)}) collective-permute-start(f32[8,1024]{1,0:T(8,128)S(1)} %concatenate.262), channel_id=1, source_target_pairs={{0,2},{2,0},{1,3},{3,1},{4,6},{6,4},{5,7},{7,5},{8,10},{10,8},{9,1... | collective-permute-start | bytes 98312 | tf_op jit(solution)/shard_map/ppermute | solution.py:127
  609.8 13.8 %collective-permute-start.73 = (bf16[3,128,256]{1,2,0:T(8,128)(2,1)S(1)}, bf16[3,128,256]{1,2,0:T(8,128)(2,1)S(1)}, u32[]{:S(2)}, u32[]{:S(2)}) collective-permute-start(bf16[3,128,256]{1,2,0:T(8,128)(2,1)S(1)} %pad_maximum_fusion.26), channel_id=1, source_target_pairs={{0,8},{8,16},{16,24},{24,28},{28,20},{20,12},{12,4},{4,0},{1,9},{9... | collective-permute-start | bytes 589832 | tf_op jit(solution)/shard_map/ppermute | solution.py:162
  624.6 50.2 %collective-permute-start.81 = (bf16[3,1024,256]{1,2,0:T(8,128)(2,1)}, bf16[3,1024,256]{1,2,0:T(8,128)(2,1)S(1)}, u32[]{:S(2)}, u32[]{:S(2)}) collective-permute-start(bf16[3,1024,256]{1,2,0:T(8,128)(2,1)} %slice.1004), channel_id=1, source_target_pairs={{0,2},{2,0},{1,3},{3,1},{4,6},{6,4},{5,7},{7,5},{8,10},{10,8},{9,1... | collective-permute-start | bytes 4718600 | tf_op jit(solution)/shard_map/ppermute | solution.py:127
  625.2 71.1 %collective-permute-start.63 = (bf16[512,1024]{1,0:T(8,128)(2,1)}, bf16[512,1024]{1,0:T(8,128)(2,1)}, u32[]{:S(2)}, u32[]{:S(2)}) collective-permute-start(bf16[512,1024]{1,0:T(8,128)(2,1)} %get-tuple-element.99), channel_id=1, source_target_pairs={{0,1},{1,0},{2,3},{3,2},{4,5},{5,4},{6,7},{7,6},{8,9},{9,8},{10,11... | collective-permute-start | bytes 3145736 | tf_op jit(solution)/shard_map/ppermute | solution.py:127
  638.9 33.8 %collective-permute-start.65 = (bf16[256,1024]{1,0:T(8,128)(2,1)S(1)}, bf16[256,1024]{1,0:T(8,128)(2,1)}, u32[]{:S(2)}, u32[]{:S(2)}) collective-permute-start(bf16[256,1024]{1,0:T(8,128)(2,1)S(1)} %add_convert_fusion.5), channel_id=1, source_target_pairs={{0,2},{2,0},{1,3},{3,1},{4,6},{6,4},{5,7},{7,5},{8,10},{10,8},{9,1... | collective-permute-start | bytes 1572872 | tf_op jit(solution)/shard_map/ppermute | solution.py:127
  649.5 25.3 %collective-permute-start.80 = (bf16[3,128,256]{1,2,0:T(8,128)(2,1)S(1)}, bf16[3,128,256]{1,2,0:T(8,128)(2,1)S(1)}, u32[]{:S(2)}, u32[]{:S(2)}) collective-permute-start(bf16[3,128,256]{1,2,0:T(8,128)(2,1)S(1)} %fusion.108), channel_id=1, source_target_pairs={{0,2},{2,0},{1,3},{3,1},{4,6},{6,4},{5,7},{7,5},{8,10},{10,8},{9,1... | collective-permute-start | bytes 589832 | tf_op jit(solution)/shard_map/ppermute | solution.py:127
  672.7 16.2 %collective-permute-start.66 = (bf16[256,1024]{1,0:T(8,128)(2,1)}, bf16[256,1024]{1,0:T(8,128)(2,1)}, u32[]{:S(2)}, u32[]{:S(2)}) collective-permute-start(bf16[256,1024]{1,0:T(8,128)(2,1)} %collective-permute-done.65), channel_id=1, source_target_pairs={{0,1},{1,0},{2,3},{3,2},{4,5},{5,4},{6,7},{7,6},{8,9},{9,8},{10,11... | collective-permute-start | bytes 1572872 | tf_op jit(solution)/shard_map/ppermute | solution.py:127
  (167 other events, 2085.6 us)
